TPU v7x, 512 devices: a whole 4x8x8 slice. The times are simulated.
512 devices in a mesh: segment: 2 (over y_hi), dp: 64 (over z, x, core), rows: 4 (over y_lo).
Axes of the slice: x: 4, y: 8 (y_hi: 2, y_lo: 4; y = y_hi * 4 + y_lo), z: 8, core: 2. Of those that a mesh axis runs over, the one named last changes fastest.
Arguments:
- section_input: bfloat16 [2, 2, 64, 20, 16, 1536], P('segment', None, 'dp', 'rows'), may hold values from -16 to 16
- adjoint_in: bfloat16 [2, 64, 20, 16, 1536], P(None, 'dp', 'rows'), may hold values from -6 to 6
- kernel: bfloat16 [2, 1, 49, 1536], P('segment', None, None, 'dp'), may hold values from -0.875 to 0.875
- conv_bias: bfloat16 [2, 1, 1536], P('segment', None, 'dp'), may hold values from -4 to 4
- ln_gain: bfloat16 [2, 1, 1536], P('segment', None, 'dp'), may hold values from 0.099609375 to 1.8984375
- ln_shift: bfloat16 [2, 1, 1536], P('segment', None, 'dp'), may hold values from -3 to 3
- layer_scale: bfloat16 [2, 1, 1536], P('segment', None, 'dp'), may hold values from 0.29882812 to 1.5
Outputs:
- section_adjoint: bfloat16 [2, 2, 64, 20, 16, 1536], P('segment', None, 'dp', 'rows')
- kernel_grad: float32 [2, 1, 49, 1536], P('segment', None, None, 'dp')
- bias_grad: float32 [2, 1, 1536], P('segment', None, 'dp')
- gain_grad: float32 [2, 1, 1536], P('segment', None, 'dp')
- shift_grad: float32 [2, 1, 1536], P('segment', None, 'dp')
- scale_grad: float32 [2, 1, 1536], P('segment', None, 'dp')
All inputs are finite; a program needn't handle non-finite values.
Results may differ from a plain program's by a relative error of at most 0.005.
Values may be sent and summed in bfloat16 or wider, within the bound.
A program may use at most 64 MiB of HBM per device.

v0:
```python
import jax
import jax.numpy as jnp
from jax import lax
from jax.sharding import PartitionSpec as P

EPSILON = 1e-06


def with_halo(cells, sides, width):
    for axis, dim in sides:
        count = lax.axis_size(axis)
        ends = count - 1
        head = lax.slice_in_dim(cells, 0, width, axis=dim)
        tail = lax.slice_in_dim(cells, cells.shape[dim] - width, cells.shape[dim], axis=dim)
        cells = jnp.concatenate(
            [
                lax.ppermute(tail, axis, [(i, (i + 1) % count) for i in range(ends)]),
                cells,
                lax.ppermute(head, axis, [((i + 1) % count, i) for i in range(ends)]),
            ],
            axis=dim,
        )
    return cells


def from_behind(value, axis, by):
    count = lax.axis_size(axis)
    pairs = [(i, i + by) for i in range(count) if 0 <= i + by < count]
    return lax.ppermute(value, axis, pairs)


def conv_sum(padded, kernel, height, width):
    total = jnp.zeros((padded.shape[0], height, width, padded.shape[3]), jnp.float32)
    for row_off in range(7):
        for col_off in range(7):
            total = (
                total
                + padded[:, row_off : row_off + height, col_off : col_off + width, :].astype(
                    jnp.float32
                )
                * kernel[row_off * 7 + col_off]
            )
    return total


def conv_adjoint(grad_pad, kernel, height, width):
    total = jnp.zeros((grad_pad.shape[0], height, width, grad_pad.shape[3]), jnp.float32)
    for row_off in range(7):
        for col_off in range(7):
            total = (
                total
                + grad_pad[
                    :, 6 - row_off : 6 - row_off + height, 6 - col_off : 6 - col_off + width, :
                ].astype(jnp.float32)
                * kernel[row_off * 7 + col_off]
            )
    return total


def kernel_terms(padded, grad_rounded, height, width):
    grad_float = grad_rounded.astype(jnp.float32)
    return jnp.stack(
        [
            jnp.sum(
                padded[:, row_off : row_off + height, col_off : col_off + width, :].astype(
                    jnp.float32
                )
                * grad_float,
                axis=(0, 1, 2),
            )
            for row_off in range(7)
            for col_off in range(7)
        ]
    )


def statistics(padded, kernel, conv_bias, ln_gain, ln_shift, height, width):
    mixed = conv_sum(padded, kernel.astype(jnp.float32), height, width) + conv_bias.astype(
        jnp.float32
    )
    average = jnp.mean(mixed, axis=-1, keepdims=True)
    centred = mixed - average
    inverse = lax.rsqrt(jnp.mean(centred * centred, axis=-1, keepdims=True) + EPSILON)
    normed = centred * inverse
    shaped = normed * ln_gain.astype(jnp.float32) + ln_shift.astype(jnp.float32)
    return (normed, inverse, shaped)


def back_local(grad_out, normed, inverse, shaped, ln_gain, layer_scale):
    upstream = grad_out.astype(jnp.float32)
    grad_scale = jnp.sum(shaped * upstream, axis=(0, 1, 2))
    grad_shaped = layer_scale.astype(jnp.float32) * upstream
    grad_shift = jnp.sum(grad_shaped, axis=(0, 1, 2))
    grad_gain = jnp.sum(grad_shaped * normed, axis=(0, 1, 2))
    grad_normed = grad_shaped * ln_gain.astype(jnp.float32)
    grad_mix = inverse * (
        grad_normed
        - jnp.mean(grad_normed, axis=-1, keepdims=True)
        - normed * jnp.mean(grad_normed * normed, axis=-1, keepdims=True)
    )
    return (upstream, grad_mix.astype(jnp.bfloat16), grad_gain, grad_shift, grad_scale)


def input_rims(current):
    widened = with_halo(current, (("rows", 1),), 3)
    return jnp.pad(widened, ((0, 0), (0, 0), (3, 3), (0, 0)))


def adjoint_rims(grad_rounded):
    widened = with_halo(grad_rounded, (("rows", 1),), 3)
    return jnp.pad(widened, ((0, 0), (0, 0), (3, 3), (0, 0)))


def local(section_input, adjoint_in, kernel, conv_bias, ln_gain, ln_shift, layer_scale):
    segments = lax.axis_size("segment")
    segment_idx = lax.axis_index("segment")
    layers = kernel.shape[1]
    micro_count = section_input.shape[1]
    images = section_input.shape[2]
    height = section_input.shape[3]
    width = section_input.shape[4]
    channels = kernel.shape[3] * lax.axis_size("dp")
    factor = 1.0 / (micro_count * images * lax.axis_size("dp"))
    totals = [jnp.zeros((layers, 49, channels), jnp.float32)] + [
        jnp.zeros((layers, channels), jnp.float32) for which in range(4)
    ]
    received = jnp.zeros(adjoint_in.shape[1:], jnp.bfloat16)
    outputs = jnp.zeros(section_input.shape[1:], jnp.bfloat16)
    steps = micro_count + segments - 1
    for step in range(steps):
        micro_idx = step - (segments - 1 - segment_idx)
        valid = jnp.logical_and(micro_idx >= 0, micro_idx < micro_count)
        picked = jnp.clip(micro_idx, 0, micro_count - 1)
        start = lax.dynamic_index_in_dim(section_input[0], picked, 0, keepdims=False)
        arriving = lax.dynamic_index_in_dim(adjoint_in, picked, 0, keepdims=False)
        grad_out = jnp.where(segment_idx == segments - 1, arriving, received)
        layer = 0
        kernel_full = lax.all_gather(kernel[0, layer], "dp", axis=1, tiled=True)
        bias_full = lax.all_gather(conv_bias[0, layer], "dp", axis=0, tiled=True)
        gain_full = lax.all_gather(ln_gain[0, layer], "dp", axis=0, tiled=True)
        shift_full = lax.all_gather(ln_shift[0, layer], "dp", axis=0, tiled=True)
        scale_full = lax.all_gather(layer_scale[0, layer], "dp", axis=0, tiled=True)
        padded = input_rims(start)
        normed, inverse, shaped = statistics(
            padded, kernel_full, bias_full, gain_full, shift_full, height, width
        )
        saved = [(padded, normed, inverse, shaped)]
        weight = jnp.where(valid, factor, 0.0).astype(jnp.float32)
        for layer in reversed(range(layers)):
            kernel_full = lax.all_gather(kernel[0, layer], "dp", axis=1, tiled=True)
            bias_full = lax.all_gather(conv_bias[0, layer], "dp", axis=0, tiled=True)
            gain_full = lax.all_gather(ln_gain[0, layer], "dp", axis=0, tiled=True)
            shift_full = lax.all_gather(ln_shift[0, layer], "dp", axis=0, tiled=True)
            scale_full = lax.all_gather(layer_scale[0, layer], "dp", axis=0, tiled=True)
            padded, normed, inverse, shaped = saved[layer]
            upstream, grad_rounded, grad_gain, grad_shift, grad_scale = back_local(
                grad_out, normed, inverse, shaped, gain_full, scale_full
            )
            grad_bias = jnp.sum(grad_rounded.astype(jnp.float32), axis=(0, 1, 2))
            grad_kernel = kernel_terms(padded, grad_rounded, height, width)
            grad_pad = adjoint_rims(grad_rounded)
            grad_out = (
                upstream + conv_adjoint(grad_pad, kernel_full.astype(jnp.float32), height, width)
            ).astype(jnp.bfloat16)
            totals[0] = totals[0].at[layer].add(weight * grad_kernel)
            totals[1] = totals[1].at[layer].add(weight * grad_bias)
            totals[2] = totals[2].at[layer].add(weight * grad_gain)
            totals[3] = totals[3].at[layer].add(weight * grad_shift)
            totals[4] = totals[4].at[layer].add(weight * grad_scale)
        outputs = jnp.where(
            valid, lax.dynamic_update_index_in_dim(outputs, grad_out, picked, 0), outputs
        )
        if step + 1 < steps:
            received = from_behind(grad_out, "segment", -1)
    summed = lax.psum((totals[0], totals[1], totals[2], totals[3], totals[4]), "rows")
    parts = (
        lax.psum_scatter(summed[0], "dp", scatter_dimension=2, tiled=True),
        lax.psum_scatter(summed[1], "dp", scatter_dimension=1, tiled=True),
        lax.psum_scatter(summed[2], "dp", scatter_dimension=1, tiled=True),
        lax.psum_scatter(summed[3], "dp", scatter_dimension=1, tiled=True),
        lax.psum_scatter(summed[4], "dp", scatter_dimension=1, tiled=True),
    )
    return (
        outputs[None],
        parts[0][None],
        parts[1][None],
        parts[2][None],
        parts[3][None],
        parts[4][None],
    )


def solution(mesh):
    placed = (
        P("segment", None, "dp", "rows", None, None),
        P(None, "dp", "rows", None, None),
        P("segment", None, None, "dp"),
        P("segment", None, "dp"),
        P("segment", None, "dp"),
        P("segment", None, "dp"),
        P("segment", None, "dp"),
    )
    return jax.shard_map(
        local,
        mesh=mesh,
        in_specs=placed,
        out_specs=(
            P("segment", None, "dp", "rows", None, None),
            P("segment", None, None, "dp"),
            P("segment", None, "dp"),
            P("segment", None, "dp"),
            P("segment", None, "dp"),
            P("segment", None, "dp"),
        ),
        check_vma=False,
    )
```

profile of v0, /device:TPU:2, one launch (start us, length us, event | category | flops | bytes accessed | tf_op | source)
XLA Modules:
  0.0 895.4 jit_solution(11062038830025314502)
XLA Ops:
  7.2 1.2 dynamic-slice_bitcast_fusion
  8.5 0.7 fusion.451
  9.2 3.5 collective-permute-start.10
  12.7 1.3 collective-permute-start.11
  14.0 4.6 collective-permute-start
  18.6 1.3 collective-permute-start.1
  19.9 4.6 collective-permute-start.5
  24.5 53.3 %all-gather = bf16[1,1,49,1536]{2,3,1,0:T(8,128)(2,1)S(1)} all-gather(bf16[1,1,49,24]{2,3,1,0:T(8,128)(2,1)S(1)} %copy-done.164), channel_id=2, replica_groups=mesh['segment'=2,'dp'=64,'rows'=4] {'dp'}, dimensions={3}, use_global_device_ids=true | all-gather | bytes 152880 | tf_op jit(solution)/shard_map/all_gather | solution.py:138
  77.8 7.8 slice_reduce_fusion.47
  85.8 7.8 slice_reduce_fusion.48
  96.1 245.0 %all-reduce.17 = (bf16[1536]{0:T(1024)(128)(2,1)S(1)}, bf16[1536]{0:T(1024)(128)(2,1)S(1)}, bf16[1536]{0:T(1024)(128)(2,1)S(1)}, bf16[1536]{0:T(1024)(128)(2,1)S(1)}) all-reduce(bf16[1536]{0:T(1024)(128)(2,1)S(1)} %dynamic-update-slice.34, ...), channel_id=3, replica_groups=mesh['segment'=2,'dp'=64,'rows'=4] {'dp'}, use_global_device_ids=true, to_apply=%add.6 | all-reduce | flops 6144 | bytes 24576
  341.7 5.1 slice_reduce_fusion.46
  346.9 1.5 collective-permute-start.6
  348.8 6.3 fusion.448
  355.3 1.0 fusion.188
  356.3 1.4 fusion.261
  357.8 1.1 fusion.262
  359.7 6.2 fusion.445
  366.0 4.6 collective-permute-start.2
  370.5 1.7 collective-permute-start.3
  372.7 0.6 add_rsqrt_fusion.1
  373.3 1.2 select_maximum_fusion.2
  374.9 6.4 fusion.442
  381.3 1.0 fusion.259
  383.1 5.4 bitcast_dynamic-update-slice_fusion.1
  388.5 0.8 copy-done
  389.3 1.3 collective-permute-start.4
  390.6 0.8 multiply_reduce_fusion
  393.2 0.6 stack.475
  396.2 0.6 stack.480
  398.5 0.6 stack.485
  399.7 0.6 stack.487
  408.7 0.6 stack.455
  411.7 0.6 stack.461
  412.9 0.6 stack.463
  414.1 0.6 stack.465
  418.2 5.9 stack.499
  424.2 1.3 add_rsqrt_fusion
  425.5 2.1 fusion.184
  427.6 1.4 fusion.335
  429.1 4.6 collective-permute-start.7
  433.6 1.3 collective-permute-start.8
  434.9 1.1 fusion.336
  436.4 4.3 collective-permute-done.8
  441.3 5.5 fusion.438
  446.8 1.4 collective-permute-start.9
  448.2 1.0 fusion.333
  451.6 6.1 stack.549
  457.7 0.8 copy.32
  458.5 1.4 collective-permute-done.9
  459.9 1.4 fusion.186
  461.3 1.4 fusion.409
  463.3 1.1 fusion.410
  464.6 0.7 copy-done.6
  465.3 1.4 fusion.407
  466.8 246.3 %all-reduce.15 = (f32[1,1536]{1,0:T(1,128)S(1)}, f32[1,1536]{1,0:T(1,128)S(1)}, f32[1,1536]{1,0:T(1,128)S(1)}, f32[1,1536]{1,0:T(1,128)}) all-reduce(f32[1,1536]{1,0:T(1,128)S(1)} %add.1453, f32[1,1536]{1,0:T(1,128)S(1)} %add.1456, f32[1,1536]{1,0:T(1,128)S(1)} %add.1459, ...), channel_id=8, replica_groups=mesh['segment'=2,'dp'=64,'rows'=4] {'dp'}, use_global_device_ids=true, to_apply=%region_165.166.clone | all-reduce | flops 6144 | bytes 49152
  715.0 7.5 collective-permute-start.12
  722.5 1.3 collective-permute-start.13
  724.5 1.7 copy.17
  726.5 0.8 constant_dynamic-slice_fusion.3
  727.3 2.3 collective-permute-done.13
  730.1 4.7 bitcast_dynamic-update-slice_fusion
  734.9 133.6 %reduce-scatter.8.cloned.1.call-done = f32[1,49,24]{1,0,2:T(1,128)} async-done(((f32[1,49,1536]{1,0,2:T(1,128)}), f32[1,49,24]{1,0,2:T(1,128)}) %reduce-scatter.8.cloned.1.call-update) | async-done | bytes 4720
  868.5 19.9 %all-reduce.16 = (f32[1,49,24]{1,0,2:T(1,128)}, f32[1,24]{1,0:T(1,128)}, f32[1,24]{1,0:T(1,128)}, f32[1,24]{1,0:T(1,128)}, f32[1,24]{1,0:T(1,128)}) all-reduce(f32[1,49,24]{1,0,2:T(1,128)} %reduce-scatter.8.cloned.1.call-done, f32[1,24]{1,0:T(1,128)S(1)} %copy-done.166, ...), channel_id=1, replica_groups=mesh['segment'=2,'dp'=64,'rows'=4] {'rows'}, use_global_device_ids=true, to_apply=%region_159.160 | all-reduce | flops 1272 | bytes 10176 | tf_op jit(solution)/shard_map/psum | solution.py:175
  (545 shorter events, 31.6 us)
Async XLA Ops:
  7.2 861.3 %reduce-scatter.8.cloned.1.call-start = ((), (), s32[]{:S(2)}) async-start(), calls=%async_computation.1 | async-start | bytes 798720
  8.5 16.0 %copy-start.164 = (bf16[1,1,49,24]{2,3,1,0:T(8,128)(2,1)S(1)}, bf16[1,1,49,24]{2,3,1,0:T(8,128)(2,1)}, u32[]{:S(2)}) copy-start(bf16[1,1,49,24]{2,3,1,0:T(8,128)(2,1)} %param.39) | copy-start | bytes 7060
  9.2 364.1 %collective-permute-start.10 = (bf16[1,3,16,1536]{3,2,1,0:T(8,128)(2,1)}, bf16[1,3,16,1536]{3,2,1,0:T(8,128)(2,1)S(1)}, u32[]{:S(2)}, u32[]{:S(2)}) collective-permute-start(bf16[1,3,16,1536]{3,2,1,0:T(8,128)(2,1)} %get-tuple-element.448), channel_id=1, source_target_pairs={{0,1},{1,2},{2,3},{4,5},{5,6},{6,7},{8,9},{9,10},{10,11},{12,13},{... | collective-permute-start | bytes 442376 | tf_op jit(solution)/shard_map/ppermute | solution.py:17
  12.7 360.6 %collective-permute-start.11 = (bf16[1,3,16,1536]{3,2,1,0:T(8,128)(2,1)}, bf16[1,3,16,1536]{3,2,1,0:T(8,128)(2,1)}, u32[]{:S(2)}, u32[]{:S(2)}) collective-permute-start(bf16[1,3,16,1536]{3,2,1,0:T(8,128)(2,1)} %get-tuple-element.449), channel_id=1, source_target_pairs={{1,0},{2,1},{3,2},{5,4},{6,5},{7,6},{9,8},{10,9},{11,10},{13,12},{... | collective-permute-start | bytes 442376 | tf_op jit(solution)/shard_map/ppermute | solution.py:19
  14.0 332.9 %collective-permute-start = (bf16[1,3,16,1536]{3,2,1,0:T(8,128)(2,1)S(1)}, bf16[1,3,16,1536]{3,2,1,0:T(8,128)(2,1)S(1)}, u32[]{:S(2)}, u32[]{:S(2)}) collective-permute-start(bf16[1,3,16,1536]{3,2,1,0:T(8,128)(2,1)S(1)} %get-tuple-element.456), channel_id=1, source_target_pairs={{0,1},{1,2},{2,3},{4,5},{5,6},{6,7},{8,9},{9,10},{10,11},{12,13},{... | collective-permute-start | bytes 442376 | tf_op jit(solution)/shard_map/ppermute | solution.py:17
  18.6 329.8 %collective-permute-start.1 = (bf16[1,3,16,1536]{3,2,1,0:T(8,128)(2,1)S(1)}, bf16[1,3,16,1536]{3,2,1,0:T(8,128)(2,1)S(1)}, u32[]{:S(2)}, u32[]{:S(2)}) collective-permute-start(bf16[1,3,16,1536]{3,2,1,0:T(8,128)(2,1)S(1)} %get-tuple-element.457), channel_id=1, source_target_pairs={{1,0},{2,1},{3,2},{5,4},{6,5},{7,6},{9,8},{10,9},{11,10},{13,12},{... | collective-permute-start | bytes 442376 | tf_op jit(solution)/shard_map/ppermute | solution.py:19
  19.9 339.1 %collective-permute-start.5 = (bf16[1,3,16,1536]{3,2,1,0:T(8,128)(2,1)S(1)}, bf16[1,3,16,1536]{3,2,1,0:T(8,128)(2,1)S(1)}, u32[]{:S(2)}, u32[]{:S(2)}) collective-permute-start(bf16[1,3,16,1536]{3,2,1,0:T(8,128)(2,1)S(1)} %get-tuple-element.452), channel_id=1, source_target_pairs={{0,1},{1,2},{2,3},{4,5},{5,6},{6,7},{8,9},{9,10},{10,11},{12,13},{... | collective-permute-start | bytes 442376 | tf_op jit(solution)/shard_map/ppermute | solution.py:17
  85.6 273.7 %copy-start.17 = (f32[1536]{0:T(1024)}, f32[1536]{0:T(1024)S(1)}, u32[]{:S(2)}) copy-start(f32[1536]{0:T(1024)S(1)} %get-tuple-element.346) | copy-start | bytes 18436
  85.6 273.7 %copy-start.20 = (f32[1536]{0:T(1024)}, f32[1536]{0:T(1024)S(1)}, u32[]{:S(2)}) copy-start(f32[1536]{0:T(1024)S(1)} %get-tuple-element.347) | copy-start | bytes 18436
  85.6 273.7 %copy-start.23 = (f32[1536]{0:T(1024)}, f32[1536]{0:T(1024)S(1)}, u32[]{:S(2)}) copy-start(f32[1536]{0:T(1024)S(1)} %get-tuple-element.348) | copy-start | bytes 18436
  85.6 273.7 %copy-start.26 = (f32[1536]{0:T(1024)}, f32[1536]{0:T(1024)S(1)}, u32[]{:S(2)}) copy-start(f32[1536]{0:T(1024)S(1)} %get-tuple-element.349) | copy-start | bytes 18436
  85.6 273.7 %copy-start.29 = (f32[1536]{0:T(1024)}, f32[1536]{0:T(1024)S(1)}, u32[]{:S(2)}) copy-start(f32[1536]{0:T(1024)S(1)} %get-tuple-element.350) | copy-start | bytes 18436
  85.7 273.7 %copy-start.32 = (f32[1536]{0:T(1024)}, f32[1536]{0:T(1024)S(1)}, u32[]{:S(2)}) copy-start(f32[1536]{0:T(1024)S(1)} %get-tuple-element.351) | copy-start | bytes 18436
  85.7 273.7 %copy-start.35 = (f32[1536]{0:T(1024)}, f32[1536]{0:T(1024)S(1)}, u32[]{:S(2)}) copy-start(f32[1536]{0:T(1024)S(1)} %get-tuple-element.352) | copy-start | bytes 18436
  85.7 273.7 %copy-start.39 = (f32[1536]{0:T(1024)}, f32[1536]{0:T(1024)S(1)}, u32[]{:S(2)}) copy-start(f32[1536]{0:T(1024)S(1)} %get-tuple-element.353) | copy-start | bytes 18436
  85.7 273.7 %copy-start.43 = (f32[1536]{0:T(1024)}, f32[1536]{0:T(1024)S(1)}, u32[]{:S(2)}) copy-start(f32[1536]{0:T(1024)S(1)} %get-tuple-element.354) | copy-start | bytes 18436
  85.7 273.7 %copy-start.47 = (f32[1536]{0:T(1024)}, f32[1536]{0:T(1024)S(1)}, u32[]{:S(2)}) copy-start(f32[1536]{0:T(1024)S(1)} %get-tuple-element.355) | copy-start | bytes 18436
  85.7 273.7 %copy-start.51 = (f32[1536]{0:T(1024)}, f32[1536]{0:T(1024)S(1)}, u32[]{:S(2)}) copy-start(f32[1536]{0:T(1024)S(1)} %get-tuple-element.356) | copy-start | bytes 18436
  85.7 273.7 %copy-start.55 = (f32[1536]{0:T(1024)}, f32[1536]{0:T(1024)S(1)}, u32[]{:S(2)}) copy-start(f32[1536]{0:T(1024)S(1)} %get-tuple-element.357) | copy-start | bytes 18436
  85.7 273.7 %copy-start.59 = (f32[1536]{0:T(1024)}, f32[1536]{0:T(1024)S(1)}, u32[]{:S(2)}) copy-start(f32[1536]{0:T(1024)S(1)} %get-tuple-element.358) | copy-start | bytes 18436
  85.7 9.3 %copy-start.168 = (bf16[1,1,24]{2,1,0:T(2,128)(2,1)S(1)}, bf16[1,1,24]{2,1,0:T(2,128)(2,1)}, u32[]{:S(2)}) copy-start(bf16[1,1,24]{2,1,0:T(2,128)(2,1)} %param.43) | copy-start | bytes 148
  85.8 9.5 %copy-start.169 = (bf16[1,1,24]{2,1,0:T(2,128)(2,1)S(1)}, bf16[1,1,24]{2,1,0:T(2,128)(2,1)}, u32[]{:S(2)}) copy-start(bf16[1,1,24]{2,1,0:T(2,128)(2,1)} %param.41) | copy-start | bytes 148
  85.8 9.8 %copy-start.170 = (bf16[1,1,24]{2,1,0:T(2,128)(2,1)S(1)}, bf16[1,1,24]{2,1,0:T(2,128)(2,1)}, u32[]{:S(2)}) copy-start(bf16[1,1,24]{2,1,0:T(2,128)(2,1)} %param.40) | copy-start | bytes 148
  85.8 10.0 %copy-start.171 = (bf16[1,1,24]{2,1,0:T(2,128)(2,1)S(1)}, bf16[1,1,24]{2,1,0:T(2,128)(2,1)}, u32[]{:S(2)}) copy-start(bf16[1,1,24]{2,1,0:T(2,128)(2,1)} %param.42) | copy-start | bytes 148
  93.6 255.1 %copy-start.119 = (f32[1536]{0:T(1024)}, f32[1536]{0:T(1024)S(1)}, u32[]{:S(2)}) copy-start(f32[1536]{0:T(1024)S(1)} %get-tuple-element.335) | copy-start | bytes 18436
  93.6 255.1 %copy-start.123 = (f32[1536]{0:T(1024)}, f32[1536]{0:T(1024)S(1)}, u32[]{:S(2)}) copy-start(f32[1536]{0:T(1024)S(1)} %get-tuple-element.336) | copy-start | bytes 18436
  93.6 255.1 %copy-start.127 = (f32[1536]{0:T(1024)}, f32[1536]{0:T(1024)S(1)}, u32[]{:S(2)}) copy-start(f32[1536]{0:T(1024)S(1)} %get-tuple-element.337) | copy-start | bytes 18436
  93.6 255.1 %copy-start.131 = (f32[1536]{0:T(1024)}, f32[1536]{0:T(1024)S(1)}, u32[]{:S(2)}) copy-start(f32[1536]{0:T(1024)S(1)} %get-tuple-element.338) | copy-start | bytes 18436
  93.6 255.1 %copy-start.135 = (f32[1536]{0:T(1024)}, f32[1536]{0:T(1024)S(1)}, u32[]{:S(2)}) copy-start(f32[1536]{0:T(1024)S(1)} %get-tuple-element.339) | copy-start | bytes 18436
  93.6 265.8 %copy-start.63 = (f32[1536]{0:T(1024)}, f32[1536]{0:T(1024)S(1)}, u32[]{:S(2)}) copy-start(f32[1536]{0:T(1024)S(1)} %get-tuple-element.321) | copy-start | bytes 18436
  93.6 265.8 %copy-start.67 = (f32[1536]{0:T(1024)}, f32[1536]{0:T(1024)S(1)}, u32[]{:S(2)}) copy-start(f32[1536]{0:T(1024)S(1)} %get-tuple-element.322) | copy-start | bytes 18436
  93.6 265.8 %copy-start.71 = (f32[1536]{0:T(1024)}, f32[1536]{0:T(1024)S(1)}, u32[]{:S(2)}) copy-start(f32[1536]{0:T(1024)S(1)} %get-tuple-element.323) | copy-start | bytes 18436
  93.6 265.8 %copy-start.75 = (f32[1536]{0:T(1024)}, f32[1536]{0:T(1024)S(1)}, u32[]{:S(2)}) copy-start(f32[1536]{0:T(1024)S(1)} %get-tuple-element.324) | copy-start | bytes 18436
  93.6 265.8 %copy-start.79 = (f32[1536]{0:T(1024)}, f32[1536]{0:T(1024)S(1)}, u32[]{:S(2)}) copy-start(f32[1536]{0:T(1024)S(1)} %get-tuple-element.325) | copy-start | bytes 18436
  93.7 265.8 %copy-start.83 = (f32[1536]{0:T(1024)}, f32[1536]{0:T(1024)S(1)}, u32[]{:S(2)}) copy-start(f32[1536]{0:T(1024)S(1)} %get-tuple-element.326) | copy-start | bytes 18436
  93.7 265.8 %copy-start.87 = (f32[1536]{0:T(1024)}, f32[1536]{0:T(1024)S(1)}, u32[]{:S(2)}) copy-start(f32[1536]{0:T(1024)S(1)} %get-tuple-element.327) | copy-start | bytes 18436
  93.7 265.8 %copy-start.91 = (f32[1536]{0:T(1024)}, f32[1536]{0:T(1024)S(1)}, u32[]{:S(2)}) copy-start(f32[1536]{0:T(1024)S(1)} %get-tuple-element.328) | copy-start | bytes 18436
  93.7 265.8 %copy-start.95 = (f32[1536]{0:T(1024)}, f32[1536]{0:T(1024)S(1)}, u32[]{:S(2)}) copy-start(f32[1536]{0:T(1024)S(1)} %get-tuple-element.329) | copy-start | bytes 18436
  93.7 265.8 %copy-start.99 = (f32[1536]{0:T(1024)}, f32[1536]{0:T(1024)S(1)}, u32[]{:S(2)}) copy-start(f32[1536]{0:T(1024)S(1)} %get-tuple-element.330) | copy-start | bytes 18436
  93.7 265.8 %copy-start.103 = (f32[1536]{0:T(1024)}, f32[1536]{0:T(1024)S(1)}, u32[]{:S(2)}) copy-start(f32[1536]{0:T(1024)S(1)} %get-tuple-element.331) | copy-start | bytes 18436
  93.7 265.8 %copy-start.107 = (f32[1536]{0:T(1024)}, f32[1536]{0:T(1024)S(1)}, u32[]{:S(2)}) copy-start(f32[1536]{0:T(1024)S(1)} %get-tuple-element.332) | copy-start | bytes 18436
  93.7 265.8 %copy-start.111 = (f32[1536]{0:T(1024)}, f32[1536]{0:T(1024)S(1)}, u32[]{:S(2)}) copy-start(f32[1536]{0:T(1024)S(1)} %get-tuple-element.333) | copy-start | bytes 18436
  93.7 265.8 %copy-start.115 = (f32[1536]{0:T(1024)}, f32[1536]{0:T(1024)S(1)}, u32[]{:S(2)}) copy-start(f32[1536]{0:T(1024)S(1)} %get-tuple-element.334) | copy-start | bytes 18436
  341.1 14.3 %copy-start.145 = (f32[1536]{0:T(1024)}, f32[1536]{0:T(1024)S(1)}, u32[]{:S(2)}) copy-start(f32[1536]{0:T(1024)S(1)} %convert_element_type.1468) | copy-start | bytes 18436
  346.9 36.2 %copy-start.139 = (f32[1536]{0:T(1024)}, f32[1536]{0:T(1024)S(1)}, u32[]{:S(2)}) copy-start(f32[1536]{0:T(1024)S(1)} %get-tuple-element.359) | copy-start | bytes 18436
  346.9 36.2 %copy-start.142 = (f32[1536]{0:T(1024)}, f32[1536]{0:T(1024)S(1)}, u32[]{:S(2)}) copy-start(f32[1536]{0:T(1024)S(1)} %get-tuple-element.360) | copy-start | bytes 18436
  346.9 12.1 %collective-permute-start.6 = (bf16[1,3,16,1536]{3,2,1,0:T(8,128)(2,1)S(1)}, bf16[1,3,16,1536]{3,2,1,0:T(8,128)(2,1)S(1)}, u32[]{:S(2)}, u32[]{:S(2)}) collective-permute-start(bf16[1,3,16,1536]{3,2,1,0:T(8,128)(2,1)S(1)} %get-tuple-element.453), channel_id=1, source_target_pairs={{1,0},{2,1},{3,2},{5,4},{6,5},{7,6},{9,8},{10,9},{11,10},{13,12},{... | collective-permute-start | bytes 442376 | tf_op jit(solution)/shard_map/ppermute | solution.py:19
  366.0 8.6 copy-start.152
  366.0 16.8 %collective-permute-start.2 = (bf16[1,3,16,1536]{3,2,1,0:T(8,128)(2,1)S(1)}, bf16[1,3,16,1536]{3,2,1,0:T(8,128)(2,1)S(1)}, u32[]{:S(2)}, u32[]{:S(2)}) collective-permute-start(bf16[1,3,16,1536]{3,2,1,0:T(8,128)(2,1)S(1)} %get-tuple-element.454), channel_id=1, source_target_pairs={{0,1},{1,2},{2,3},{4,5},{5,6},{6,7},{8,9},{9,10},{10,11},{12,13},{... | collective-permute-start | bytes 442376 | tf_op jit(solution)/shard_map/ppermute | solution.py:17
  370.5 12.2 %collective-permute-start.3 = (bf16[1,3,16,1536]{3,2,1,0:T(8,128)(2,1)S(1)}, bf16[1,3,16,1536]{3,2,1,0:T(8,128)(2,1)S(1)}, u32[]{:S(2)}, u32[]{:S(2)}) collective-permute-start(bf16[1,3,16,1536]{3,2,1,0:T(8,128)(2,1)S(1)} %get-tuple-element.455), channel_id=1, source_target_pairs={{1,0},{2,1},{3,2},{5,4},{6,5},{7,6},{9,8},{10,9},{11,10},{13,12},{... | collective-permute-start | bytes 442376 | tf_op jit(solution)/shard_map/ppermute | solution.py:19
  381.3 9.3 %copy-start.150 = (f32[5,16]{1,0:T(8,128)}, f32[5,16]{1,0:T(8,128)S(1)}, u32[]{:S(2)}) copy-start(f32[5,16]{1,0:T(8,128)S(1)} %broadcast_multiply_fusion.2) | copy-start | bytes 964
  389.3 36.2 %collective-permute-start.4 = (bf16[1,5,16,1536]{3,2,1,0:T(8,128)(2,1)}, bf16[1,5,16,1536]{3,2,1,0:T(8,128)(2,1)}, u32[]{:S(2)}, u32[]{:S(2)}) collective-permute-start(bf16[1,5,16,1536]{3,2,1,0:T(8,128)(2,1)} %get-tuple-element.440), channel_id=1, source_target_pairs={{256,0},{257,1},{258,2},{259,3},{260,4},{261,5},{262,6},{263,7},{2... | collective-permute-start | bytes 737288 | tf_op jit(solution)/shard_map/ppermute | solution.py:29
  391.4 34.1 %copy-start.146 = (f32[1536]{0:T(1024)S(1)}, f32[1536]{0:T(1024)}, u32[]{:S(2)}) copy-start(f32[1536]{0:T(1024)} %copy-done.145) | copy-start | bytes 18436
  391.4 34.1 %copy-start.153 = (f32[5,16]{1,0:T(8,128)S(1)}, f32[5,16]{1,0:T(8,128)}, u32[]{:S(2)}) copy-start(f32[5,16]{1,0:T(8,128)} %copy-done.152) | copy-start | bytes 964
  391.4 34.1 %copy-start.155 = (f32[5,16]{1,0:T(8,128)S(1)}, f32[5,16]{1,0:T(8,128)}, u32[]{:S(2)}) copy-start(f32[5,16]{1,0:T(8,128)} %add_rsqrt_fusion.1) | copy-start | bytes 964
  429.1 7.3 collective-permute-start.7
  433.6 7.0 collective-permute-start.8
  446.8 13.1 %collective-permute-start.9 = (bf16[1,5,16,1536]{3,2,1,0:T(8,128)(2,1)}, bf16[1,5,16,1536]{3,2,1,0:T(8,128)(2,1)}, u32[]{:S(2)}, u32[]{:S(2)}) collective-permute-start(bf16[1,5,16,1536]{3,2,1,0:T(8,128)(2,1)} %get-tuple-element.435), channel_id=1, source_target_pairs={{256,0},{257,1},{258,2},{259,3},{260,4},{261,5},{262,6},{263,7},{2... | collective-permute-start | bytes 737288 | tf_op jit(solution)/shard_map/ppermute | solution.py:29
  466.7 257.6 %copy-start.4 = (f32[1,49,1536]{2,1,0:T(8,128)S(1)}, f32[1,49,1536]{2,1,0:T(8,128)}, u32[]{:S(2)}) copy-start(f32[1,49,1536]{2,1,0:T(8,128)} %stack.549) | copy-start | bytes 903172
  715.0 12.3 %collective-permute-start.12 = (bf16[1,3,16,1536]{3,2,1,0:T(8,128)(2,1)S(1)}, bf16[1,3,16,1536]{3,2,1,0:T(8,128)(2,1)S(1)}, u32[]{:S(2)}, u32[]{:S(2)}) collective-permute-start(bf16[1,3,16,1536]{3,2,1,0:T(8,128)(2,1)S(1)} %get-tuple-element.446), channel_id=1, source_target_pairs={{0,1},{1,2},{2,3},{4,5},{5,6},{6,7},{8,9},{9,10},{10,11},{12,13},{... | collective-permute-start | bytes 442376 | tf_op jit(solution)/shard_map/ppermute | solution.py:17
  722.5 7.0 collective-permute-start.13
  730.1 138.4 %copy-start.166 = (f32[1,24]{1,0:T(1,128)S(1)}, f32[1,24]{1,0:T(1,128)}, u32[]{:S(2)}) copy-start(f32[1,24]{1,0:T(1,128)} %constant_dynamic-slice_fusion.2) | copy-start | bytes 292
  730.1 138.3 %copy-start.167 = (f32[1,24]{1,0:T(1,128)S(1)}, f32[1,24]{1,0:T(1,128)}, u32[]{:S(2)}) copy-start(f32[1,24]{1,0:T(1,128)} %constant_dynamic-slice_fusion.1) | copy-start | bytes 292
  734.9 153.5 %copy-start.16 = (bf16[1,2,1,5,16,1536]{5,4,3,2,1,0:T(8,128)(2,1)}, bf16[1,2,1,5,16,1536]{5,4,3,2,1,0:T(8,128)(2,1)S(1)}, u32[]{:S(2)}) copy-start(bf16[1,2,1,5,16,1536]{5,4,3,2,1,0:T(8,128)(2,1)S(1)} %bitcast_dynamic-update-slice_fusion) | copy-start | bytes 1474564
  (123 other events, 476.8 us)
Sparse Core Ops, SparseCore 0:
  726.3 142.0 reduce-scatter.7
where the time goes:
time: 906 us; the launch traced here: 895 us
  blocking collectives  564 us (62%)
  waiting for transfers between devices  142 us (16%)
  local copies, waits for them, and re-layouts  72.5 us (8%)
  other arithmetic  57.2 us (6%)
  starting transfers between devices  40.3 us (4%)
  between operations  19.3 us (2%)
    unnamed x2, blocking collectives  491 us
    unnamed x2, waiting for transfers between devices  134 us
    all_gather x1, blocking collectives, local(): kernel_full = lax.all_gather(kernel[0, layer], 'dp', axis=1, tiled=True)  53.3 us
    another operation x150, local copies, waits for them, and re-layouts, kernel_terms(): jnp.stack([jnp.sum(padded[:, row_off:row_off + height, col_off:col_off +...  41.2 us
    ppermute x6, starting transfers between devices, with_halo(): lax.ppermute(tail, axis, [(i, (i + 1) % count) for i in range(ends)])  29.2 us
    slice x3, local copies, waits for them, and re-layouts, conv_sum(): kernel[row_off * 7 + col_off]  20.7 us
    psum x1, blocking collectives, local(): lax.psum((totals[0], totals[1], totals[2], totals[3], totals[4]), 'rows')  19.9 us
    reduce_sum x3, other arithmetic, statistics(): average = jnp.mean(mixed, axis=-1, keepdims=True)  18.9 us
  transfers between devices with their start and end apart: 15, of which 4 were waited for; matrix products, arithmetic and copies ran while one was open for 11% of the time, Pallas kernels for 0%

commit v1 on v0

v1 whole, which is shorter than its diff:
```python
import functools

import jax
import jax.numpy as jnp
from jax import lax
from jax.experimental import pallas as pl
from jax.experimental.pallas import tpu as pltpu
from jax.sharding import PartitionSpec as P

MESH = pl.DeviceIdType.MESH
EPSILON = 1e-06
F32 = jnp.float32
BF16 = jnp.bfloat16
LANES = 128
OFF = 8
CORES = 2
XS = 4
TAPS = 49
BIAS, GAIN, SHIFT, SCALE = 49, 50, 51, 52
SUM_G, SUM_GN, SUM_MIX = 49, 50, 51


def body(
    geometry,
    x_ref,
    adj_ref,
    kern_ref,
    bias_ref,
    gain_ref,
    shift_ref,
    scale_ref,
    out_ref,
    kgrad_ref,
    bgrad_ref,
    ggrad_ref,
    sgrad_ref,
    lgrad_ref,
    stage,
    own,
    gathered,
    by_channel,
    weights,
    xbuf,
    xhalo,
    xpad,
    mixed,
    gbuf,
    gmix,
    ghalo,
    gpad,
    stats,
    kacc,
    terms,
    flat,
    pieces,
    got1,
    sum1,
    got2,
    sum2,
    got3,
    local_sem,
    z_send,
    z_recv,
    x_send,
    x_recv,
    c_send,
    c_recv,
    xh_send,
    xh_recv,
    gh_send,
    gh_recv,
    seg_send,
    seg_recv,
    r1_send,
    r1_recv,
    r2_send,
    r2_recv,
    r3_send,
    r3_recv,
):
    zs, xs_count, rows, cpd, chunks, height, width = geometry
    xcs = xs_count * CORES
    channels = chunks * LANES
    seg = lax.axis_index("segment")
    dp = lax.axis_index("dp")
    row = lax.axis_index("rows")
    z = dp // xcs
    xc = dp % xcs
    x = xc // CORES
    core = xc % CORES
    zz = z % rows

    def dp_of(z_at, xc_at):
        return z_at * xcs + xc_at

    def remote(src, dst, send, recv, **where):
        return pltpu.make_async_remote_copy(
            src_ref=src, dst_ref=dst, send_sem=send, recv_sem=recv, device_id=where, device_id_type=MESH
        )

    barrier = pltpu.get_barrier_semaphore()

    def greet(**where):
        pl.semaphore_signal(barrier, inc=1, device_id=where, device_id_type=MESH)

    def own_x(m):
        return pltpu.make_async_copy(x_ref.at[m], xbuf.at[m], local_sem.at[m])

    def own_adj(m):
        return pltpu.make_async_copy(adj_ref.at[m], gbuf.at[m], local_sem.at[2 + m])

    for m in range(2):
        own_x(m).start()

    for k in range(1, zs):
        greet(dp=dp_of((z + k) % zs, xc))
    for k in range(1, xcs):
        greet(dp=dp_of(z, (xc + k) % xcs))
    for k in range(1, rows):
        greet(rows=(row + k) % rows)
    greet(segment=1 - seg)
    for k in range(zs):
        if k == 0:

            @pl.when(row != zz)
            def _():
                greet(rows=zz)
        else:
            greet(dp=dp_of((z + k) % zs, xc), rows=zz)

    stage[...] = jnp.zeros_like(stage)
    stage[BIAS : BIAS + 1, 0:cpd] = bias_ref[...].astype(F32)
    stage[GAIN : GAIN + 1, 0:cpd] = gain_ref[...].astype(F32)
    stage[SHIFT : SHIFT + 1, 0:cpd] = shift_ref[...].astype(F32)
    stage[SCALE : SCALE + 1, 0:cpd] = scale_ref[...].astype(F32)
    vectors = jnp.transpose(stage[...])[0:32]
    own[...] = jnp.zeros_like(own)
    own[0:cpd, 0:TAPS] = kern_ref[...].astype(F32)
    gathered[z, x, core] = (vectors + own[...]).astype(BF16)

    known = (zs - 1) + (xcs - 1) + (rows - 1) + 1 + zs

    @pl.when(row != zz)
    def _():
        pl.semaphore_wait(barrier, known)

    @pl.when(row == zz)
    def _():
        pl.semaphore_wait(barrier, known - 1)

    def z_copy(k):
        return remote(
            gathered.at[z, x, core],
            gathered.at[z, x, core],
            z_send.at[k - 1],
            z_recv.at[z],
            dp=dp_of((z + k) % zs, xc),
        )

    def z_arrival(k):
        src = (z + k) % zs
        return remote(
            gathered.at[src, x, core], gathered.at[src, x, core], z_send.at[k - 1], z_recv.at[src], dp=dp_of(src, xc)
        )

    def x_copy(k):
        return remote(
            gathered.at[:, x, core],
            gathered.at[:, x, core],
            x_send.at[k - 1],
            x_recv.at[x],
            dp=dp_of(z, ((x + k) % xs_count) * CORES + core),
        )

    def x_arrival(k):
        src = (x + k) % xs_count
        return remote(
            gathered.at[:, src, core],
            gathered.at[:, src, core],
            x_send.at[k - 1],
            x_recv.at[src],
            dp=dp_of(z, src * CORES + core),
        )

    def c_copy(k):
        src = (x + k) % xs_count
        return remote(
            gathered.at[:, src, core],
            gathered.at[:, src, core],
            c_send.at[k],
            c_recv.at[src],
            dp=dp_of(z, x * CORES + 1 - core),
        )

    def c_arrival(k):
        src = (x + k) % xs_count
        return remote(
            gathered.at[:, src, 1 - core],
            gathered.at[:, src, 1 - core],
            c_send.at[k],
            c_recv.at[src],
            dp=dp_of(z, x * CORES + 1 - core),
        )

    for k in range(1, zs):
        z_copy(k).start()

    def x_down(m):
        return remote(x_ref.at[m, height - 3 : height], xhalo.at[m, 0], xh_send.at[m, 0], xh_recv.at[m, 0], rows=(row + 1) % rows)

    def x_up(m):
        return remote(x_ref.at[m, 0:3], xhalo.at[m, 1], xh_send.at[m, 1], xh_recv.at[m, 1], rows=(row + rows - 1) % rows)

    def g_down(m):
        return remote(gmix.at[m, height - 3 : height], ghalo.at[m, 0], gh_send.at[m, 0], gh_recv.at[m, 0], rows=(row + 1) % rows)

    def g_up(m):
        return remote(gmix.at[m, 0:3], ghalo.at[m, 1], gh_send.at[m, 1], gh_recv.at[m, 1], rows=(row + rows - 1) % rows)

    for m in range(2):

        @pl.when(row < rows - 1)
        def _():
            x_down(m).start()

        @pl.when(row > 0)
        def _():
            x_up(m).start()

    @pl.when(seg == 1)
    def _():
        for m in range(2):
            own_adj(m).start()

    def clear(ch, carry):
        for m in range(2):
            for ref in (xpad, gpad):
                ref[m, ch, :, 0:OFF, :] = jnp.zeros((height + 6, OFF, LANES), F32)
                ref[m, ch, :, OFF + width : 2 * OFF + width, :] = jnp.zeros((height + 6, OFF, LANES), F32)
                ref[m, ch, 0:3, OFF : OFF + width, :] = jnp.zeros((3, width, LANES), F32)
                ref[m, ch, height + 3 : height + 6, OFF : OFF + width, :] = jnp.zeros((3, width, LANES), F32)
        return carry

    lax.fori_loop(0, chunks, clear, 0)

    for m in range(2):
        own_x(m).wait()

    def lanes_of(ch):
        return pl.ds(pl.multiple_of(ch * LANES, LANES), LANES)

    def widen(ch, carry):
        for m in range(2):
            xpad[m, ch, 3 : 3 + height, OFF : OFF + width, :] = xbuf[m, :, :, lanes_of(ch)].astype(F32)
        return carry

    lax.fori_loop(0, chunks, widen, 0)

    for k in range(1, zs):
        z_arrival(k).wait_recv()
    for k in range(1, xs_count):
        x_copy(k).start()
    c_copy(0).start()
    for k in range(1, xs_count):
        x_arrival(k).wait_recv()
        c_copy(k).start()
    for k in range(xs_count):
        c_arrival(k).wait_recv()

    def place(d, carry):
        block = gathered[d // xcs, (d % xcs) // CORES, d % CORES].astype(F32)
        by_channel[pl.ds(pl.multiple_of(d * cpd, 8), cpd), :] = block[0:cpd]
        return carry

    lax.fori_loop(0, zs * xcs, place, 0)

    def turn(ch, carry):
        block = by_channel[pl.ds(pl.multiple_of(ch * LANES, LANES), LANES), :]
        weights[ch] = jnp.transpose(block)[0:64]
        return carry

    lax.fori_loop(0, chunks, turn, 0)

    def put_halo(pad, halo, m, side, start):
        def one(ch, carry):
            pad[m, ch, start : start + 3, OFF : OFF + width, :] = halo[m, side, :, :, lanes_of(ch)].astype(F32)
            return carry

        lax.fori_loop(0, chunks, one, 0)

    def par(ch, which):
        return weights[ch, which : which + 1, :][None]

    inverse_count = 1.0 / channels

    def forward(m, carry):
        @pl.when(row > 0)
        def _():
            x_down(m).wait_recv()
            put_halo(xpad, xhalo, m, 0, 0)

        @pl.when(row < rows - 1)
        def _():
            x_up(m).wait_recv()
            put_halo(xpad, xhalo, m, 1, 3 + height)

        def conv(ch, total):
            acc = jnp.zeros((height, width, LANES), F32) + par(ch, BIAS)
            for c in range(7):
                shifted = xpad[m, ch, :, OFF - 3 + c : OFF - 3 + c + width, :]
                for r in range(7):
                    acc = acc + shifted[r : r + height] * par(ch, 7 * r + c)
            mixed[m, ch] = acc
            return total + acc

        total = lax.fori_loop(0, chunks, conv, jnp.zeros((height, width, LANES), F32))
        mean = jnp.sum(total, axis=-1, keepdims=True) * inverse_count

        def spread(ch, total):
            centred = mixed[m, ch] - mean
            return total + centred * centred

        squares = lax.fori_loop(0, chunks, spread, jnp.zeros((height, width, LANES), F32))
        variance = jnp.sum(squares, axis=-1, keepdims=True) * inverse_count
        inverse = lax.rsqrt(variance + EPSILON)
        stats[m, 0] = jnp.broadcast_to(mean, (height, width, LANES))
        stats[m, 1] = jnp.broadcast_to(inverse, (height, width, LANES))
        return carry

    lax.fori_loop(0, 2, forward, 0)

    def folded(value):
        flat_rows = jnp.sum(value, axis=0)
        total = flat_rows[0:8]
        for at in range(8, width, 8):
            total = total + flat_rows[at : at + 8]
        return total

    def seg_copy(m):
        return remote(out_ref.at[m], gbuf.at[m], seg_send.at[m], seg_recv.at[m], segment=1 - seg)

    def keep(m, ch, which, value):
        @pl.when(m == 0)
        def _():
            kacc[ch, which] = value

        @pl.when(m != 0)
        def _():
            kacc[ch, which] = kacc[ch, which] + value

    def norm_back(m):
        @pl.when(seg == 1)
        def _():
            own_adj(m).wait()

        @pl.when(seg == 0)
        def _():
            seg_copy(m).wait_recv()

        mean = stats[m, 0]
        inverse = stats[m, 1]

        def first(ch, sums):
            normed = (mixed[m, ch] - mean) * inverse
            mixed[m, ch] = normed
            upstream = gbuf[m, :, :, lanes_of(ch)].astype(F32)
            both = upstream * normed
            keep(m, ch, SUM_G, folded(upstream))
            keep(m, ch, SUM_GN, folded(both))
            factor = par(ch, SCALE) * par(ch, GAIN)
            return sums[0] + upstream * factor, sums[1] + both * factor

        zero = jnp.zeros((height, width, LANES), F32)
        plain, weighted = lax.fori_loop(0, chunks, first, (zero, zero))
        plain = jnp.sum(plain, axis=-1, keepdims=True) * inverse_count
        weighted = jnp.sum(weighted, axis=-1, keepdims=True) * inverse_count

        def second(ch, carry):
            upstream = gbuf[m, :, :, lanes_of(ch)].astype(F32)
            factor = par(ch, SCALE) * par(ch, GAIN)
            grad = inverse * (upstream * factor - plain - mixed[m, ch] * weighted)
            rounded = grad.astype(BF16)
            gmix[m, :, :, lanes_of(ch)] = rounded
            again = rounded.astype(F32)
            gpad[m, ch, 3 : 3 + height, OFF : OFF + width, :] = again
            keep(m, ch, SUM_MIX, folded(again))
            return carry

        lax.fori_loop(0, chunks, second, 0)

        @pl.when(row < rows - 1)
        def _():
            g_down(m).start()

        @pl.when(row > 0)
        def _():
            g_up(m).start()

    def adjoint(m):
        @pl.when(row > 0)
        def _():
            g_down(m).wait_recv()
            put_halo(gpad, ghalo, m, 0, 0)

        @pl.when(row < rows - 1)
        def _():
            g_up(m).wait_recv()
            put_halo(gpad, ghalo, m, 1, 3 + height)

        def conv(ch, carry):
            acc = gbuf[m, :, :, lanes_of(ch)].astype(F32)
            for c in range(7):
                shifted = gpad[m, ch, :, OFF + 3 - c : OFF + 3 - c + width, :]
                for r in range(7):
                    acc = acc + shifted[6 - r : 6 - r + height] * par(ch, 7 * r + c)
            out_ref[m, :, :, lanes_of(ch)] = acc.astype(BF16)
            return carry

        lax.fori_loop(0, chunks, conv, 0)

        @pl.when(seg == 1)
        def _():
            seg_copy(m).start()

    def r1_copy(k):
        to = (xc + k) % xcs
        return remote(pieces.at[:, to], got1.at[xc], r1_send.at[k - 1], r1_recv.at[xc], dp=dp_of(z, to))

    def r1_arrival(k):
        src = (xc + k) % xcs
        return remote(pieces.at[:, src], got1.at[src], r1_send.at[k - 1], r1_recv.at[src], dp=dp_of(z, src))

    def taps(m):
        def one(ch, carry):
            grad = gpad[m, ch, 3 : 3 + height, OFF : OFF + width, :]
            for c in range(7):
                shifted = xpad[m, ch, :, OFF - 3 + c : OFF - 3 + c + width, :]
                for r in range(7):
                    keep(m, ch, 7 * r + c, folded(shifted[r : r + height] * grad))
            return carry

        lax.fori_loop(0, chunks, one, 0)

        @pl.when(m == 1)
        def _():
            def total(ch, carry):
                terms[ch] = jnp.zeros((64, LANES), F32)
                for t in range(TAPS + 3):
                    terms[ch, t : t + 1, :] = jnp.sum(kacc[ch, t], axis=0, keepdims=True)
                return carry

            lax.fori_loop(0, chunks, total, 0)
            half = chunks // 2

            def turn_back(ch, carry):
                block = jnp.concatenate([terms[ch], terms[half + ch]], axis=0)
                flat[pl.ds(pl.multiple_of(ch * LANES, LANES), LANES), :] = jnp.transpose(block)
                return carry

            lax.fori_loop(0, half, turn_back, 0)

            def cut(d, carry):
                pieces[d // xcs, d % xcs] = flat[pl.ds(pl.multiple_of(d * cpd, 8), cpd), :]
                return carry

            lax.fori_loop(0, rows * xcs, cut, 0)
            for k in range(1, xcs):
                r1_copy(k).start()

    def step(at, carry):
        m = seg * (at % 2) + (1 - seg) * (at // 3)
        is_norm = seg * (at // 2) + (1 - seg) * (at % 3)
        is_taps = seg * (at // 4) + (1 - seg) * (at % 3 % 2)
        is_adj = seg * (at // 2 % 2) + (1 - seg) * (at % 3 // 2)

        @pl.when(is_norm == 0)
        def _():
            norm_back(m)

        @pl.when(is_taps == 1)
        def _():
            taps(m)

        @pl.when(is_adj == 1)
        def _():
            adjoint(m)

        return carry

    lax.fori_loop(0, 6, step, 0)

    for k in range(1, xcs):
        r1_arrival(k).wait_recv()
    got1[xc] = pieces[:, xc]
    acc = got1[0]
    for k in range(1, xcs):
        acc = acc + got1[k]
    sum1[...] = acc

    def r2_copy(k):
        to = (row + k) % rows
        return remote(sum1.at[to], got2.at[row], r2_send.at[k - 1], r2_recv.at[row], rows=to)

    def r2_arrival(k):
        src = (row + k) % rows
        return remote(sum1.at[src], got2.at[src], r2_send.at[k - 1], r2_recv.at[src], rows=src)

    for k in range(1, rows):
        r2_copy(k).start()
    got2[row] = sum1[row]
    for k in range(1, rows):
        r2_arrival(k).wait_recv()
    acc = got2[0]
    for k in range(1, rows):
        acc = acc + got2[k]
    sum2[...] = acc

    def r3_copy(half, k):
        to_z = half * rows + row
        return remote(sum2, got3.at[z], r3_send.at[half, k], r3_recv.at[z], dp=dp_of(to_z, xc), rows=(row + k) % rows)

    def r3_arrival(k):
        src = (z + k) % zs
        return remote(sum2, got3.at[src], r3_send.at[0, 0], r3_recv.at[src], dp=dp_of(src, xc), rows=zz)

    for half in range(2):
        for k in range(rows):
            if k == 0:

                @pl.when(z != half * rows + row)
                def _():
                    r3_copy(half, 0).start()
            else:
                r3_copy(half, k).start()

    @pl.when(row == zz)
    def _():
        got3[z] = sum2[...]

    @pl.when(row != zz)
    def _():
        r3_arrival(0).wait_recv()

    for k in range(1, zs):
        r3_arrival(k).wait_recv()
    acc = got3[0]
    for k in range(1, zs):
        acc = acc + got3[k]
    stage[...] = jnp.zeros_like(stage)
    stage[0:cpd, :] = acc
    turned = jnp.transpose(stage[...])
    upper = (z // rows) == 1
    scale_by = 1.0 / (2 * zs * xcs)
    final = jnp.where(upper, turned[64:128], turned[0:64]) * scale_by
    kgrad_ref[...] = (jnp.where(upper, pltpu.roll(acc, 64, 1), acc) * scale_by)[:, 0:TAPS]
    sum_g = final[SUM_G : SUM_G + 1, 0:cpd]
    sum_gn = final[SUM_GN : SUM_GN + 1, 0:cpd]
    bgrad_ref[...] = final[SUM_MIX : SUM_MIX + 1, 0:cpd]
    own_scale = scale_ref[...].astype(F32)
    ggrad_ref[...] = own_scale * sum_gn
    sgrad_ref[...] = own_scale * sum_g
    lgrad_ref[...] = gain_ref[...].astype(F32) * sum_gn + shift_ref[...].astype(F32) * sum_g

    for k in range(1, zs):
        z_copy(k).wait_send()
    for k in range(1, xs_count):
        x_copy(k).wait_send()
    for k in range(xs_count):
        c_copy(k).wait_send()
    for m in range(2):

        @pl.when(row < rows - 1)
        def _():
            x_down(m).wait_send()
            g_down(m).wait_send()

        @pl.when(row > 0)
        def _():
            x_up(m).wait_send()
            g_up(m).wait_send()

        @pl.when(seg == 1)
        def _():
            seg_copy(m).wait_send()

    for k in range(1, xcs):
        r1_copy(k).wait_send()
    for k in range(1, rows):
        r2_copy(k).wait_send()
    for half in range(2):
        for k in range(rows):
            if k == 0:

                @pl.when(z != half * rows + row)
                def _():
                    r3_copy(half, 0).wait_send()
            else:
                r3_copy(half, k).wait_send()


def local(xs_count, section_input, adjoint_in, kernel, conv_bias, ln_gain, ln_shift, layer_scale):
    _, micros, images, height, width, channels = section_input.shape
    cpd = kernel.shape[3]
    rows = lax.axis_size("rows")
    zs = lax.axis_size("dp") // (xs_count * CORES)
    xcs = xs_count * CORES
    chunks = channels // LANES
    vmem = pl.BlockSpec(memory_space=pltpu.VMEM)
    hbm = pl.BlockSpec(memory_space=pl.ANY)
    vec = jax.ShapeDtypeStruct((1, cpd), F32)
    dma = pltpu.SemaphoreType.DMA
    scratch = [
        pltpu.VMEM((LANES, LANES), F32),
        pltpu.VMEM((32, LANES), F32),
        pltpu.VMEM((zs, xs_count, CORES, 32, LANES), BF16),
        pltpu.VMEM((channels, LANES), F32),
        pltpu.VMEM((chunks, 64, LANES), F32),
        pltpu.VMEM((2, height, width, channels), BF16),
        pltpu.VMEM((2, 2, 3, width, channels), BF16),
        pltpu.VMEM((2, chunks, height + 6, width + 2 * OFF, LANES), F32),
        pltpu.VMEM((2, chunks, height, width, LANES), F32),
        pltpu.VMEM((2, height, width, channels), BF16),
        pltpu.VMEM((2, height, width, channels), BF16),
        pltpu.VMEM((2, 2, 3, width, channels), BF16),
        pltpu.VMEM((2, chunks, height + 6, width + 2 * OFF, LANES), F32),
        pltpu.VMEM((2, 2, height, width, LANES), F32),
        pltpu.VMEM((chunks, TAPS + 3, 8, LANES), F32),
        pltpu.VMEM((chunks, 64, LANES), F32),
        pltpu.VMEM((channels // 2, LANES), F32),
        pltpu.VMEM((rows, xcs, cpd, LANES), F32),
        pltpu.VMEM((xcs, rows, cpd, LANES), F32),
        pltpu.VMEM((rows, cpd, LANES), F32),
        pltpu.VMEM((rows, cpd, LANES), F32),
        pltpu.VMEM((cpd, LANES), F32),
        pltpu.VMEM((zs, cpd, LANES), F32),
        dma((4,)),
        dma((zs,)),
        dma((zs,)),
        dma((xs_count,)),
        dma((xs_count,)),
        dma((xs_count,)),
        dma((xs_count,)),
        dma((2, 2)),
        dma((2, 2)),
        dma((2, 2)),
        dma((2, 2)),
        dma((2,)),
        dma((2,)),
        dma((xcs,)),
        dma((xcs,)),
        dma((rows,)),
        dma((rows,)),
        dma((2, rows)),
        dma((zs,)),
    ]
    found = pl.pallas_call(
        functools.partial(body, (zs, xs_count, rows, cpd, chunks, height, width)),
        out_shape=(
            jax.ShapeDtypeStruct((micros, height, width, channels), BF16),
            jax.ShapeDtypeStruct((cpd, TAPS), F32),
            vec,
            vec,
            vec,
            vec,
        ),
        in_specs=[hbm, hbm] + [vmem] * 5,
        out_specs=(vmem,) * 6,
        scratch_shapes=scratch,
        compiler_params=pltpu.CompilerParams(
            collective_id=0, has_side_effects=True, vmem_limit_bytes=48 * 1024 * 1024
        ),
    )(
        section_input.reshape(micros, height, width, channels),
        adjoint_in.reshape(micros, height, width, channels),
        kernel.reshape(TAPS, cpd).T,
        conv_bias.reshape(1, cpd),
        ln_gain.reshape(1, cpd),
        ln_shift.reshape(1, cpd),
        layer_scale.reshape(1, cpd),
    )
    adjoint, kgrad, bgrad, ggrad, sgrad, lgrad = found
    return (
        adjoint.reshape(section_input.shape),
        kgrad.T.reshape(kernel.shape),
        bgrad.reshape(conv_bias.shape),
        ggrad.reshape(conv_bias.shape),
        sgrad.reshape(conv_bias.shape),
        lgrad.reshape(conv_bias.shape),
    )


def solution(mesh, xs_count=XS):
    placed = (
        P("segment", None, "dp", "rows", None, None),
        P(None, "dp", "rows", None, None),
        P("segment", None, None, "dp"),
        P("segment", None, "dp"),
        P("segment", None, "dp"),
        P("segment", None, "dp"),
        P("segment", None, "dp"),
    )
    return jax.shard_map(
        functools.partial(local, xs_count),
        mesh=mesh,
        in_specs=placed,
        out_specs=(placed[0],) + (placed[2],) + (placed[3],) * 4,
        check_vma=False,
    )
```

time: 906 us -> 103 us (0.11)
  the two profiles are of different devices: /device:TPU:2 before, /device:TPU:8 now
where the time goes in v1:
time: 103 us
  Pallas kernels  96.2 us (93%)
  local copies, waits for them, and re-layouts  6.16 us (6%)
    pallas_call x1, Pallas kernels, local(): pl.pallas_call(functools.partial(body, (zs, xs_count, rows, cpd, chunks,...  96.2 us
    unnamed x20, local copies, waits for them, and re-layouts  6.16 us

profile of v1, /device:TPU:8, one launch (start us, length us, event | category | flops | bytes accessed | tf_op | source)
XLA Modules:
  0.0 103.0 jit_solution(9271645650206667607)
XLA Ops:
  0.6 0.0 copy-start.2
  0.6 0.0 copy-start.6
  0.7 0.0 copy-start.3
  0.7 0.0 copy-start.4
  0.7 0.0 copy-start.5
  0.7 0.6 copy-done.2
  1.3 0.0 copy-done.6
  1.3 0.0 copy-done.3
  1.3 0.0 copy-done.4
  1.3 0.0 copy-done.5
  1.4 0.0 copy-start
  1.4 1.0 copy-done
  2.4 0.0 copy-start.1
  2.4 1.0 copy-done.1
  3.4 96.2 %shard_map.118 = (bf16[2,5,16,1536]{3,2,1,0:T(8,128)(2,1)S(1)}, f32[24,49]{1,0:T(8,128)S(1)}, f32[1,24]{1,0:T(1,128)S(1)}, f32[1,24]{1,0:T(1,128)S(1)}, f32[1,24]{1,0:T(1,128)S(1)}, /*index=5*/f32[1,24]{1,0:T(1,128)S(1)}) custom-call(bf16[2,5,16,1536]{3,2,1,0:T(8,128)(2,1)S(1)} %bitcast.19, bf16[2,5,16,1536]{3,2,1,0:T(8,128)(2,1)S(1)} %bitcast.20, ...), custom_call_target="tpu_custom_call" | custom-call | tf_op jit(solution)/shard_map/pallas_call | solution.py:656
  99.6 0.8 copy.20
  100.4 0.6 copy.21
  101.0 0.5 copy.22
  101.5 0.5 copy.23
  102.0 0.5 copy.24
  102.5 0.5 copy.25
Async XLA Ops:
  0.6 0.7 copy-start.2
  0.6 0.7 copy-start.6
  0.7 0.7 copy-start.3
  0.7 0.7 copy-start.4
  0.7 0.7 copy-start.5
  1.4 1.0 copy-start
  2.4 1.0 copy-start.1

commit v2 on v1

v2 whole, which is shorter than its diff:
```python
import functools

import jax
import jax.numpy as jnp
from jax import lax
from jax.experimental import pallas as pl
from jax.experimental.pallas import tpu as pltpu
from jax.sharding import PartitionSpec as P

MESH = pl.DeviceIdType.MESH
EPSILON = 1e-06
F32 = jnp.float32
BF16 = jnp.bfloat16
LANES = 128
OFF = 8
CORES = 2
XS = 4
TAPS = 49
BIAS, GAIN, SHIFT, SCALE = 49, 50, 51, 52
SUM_G, SUM_GN, SUM_MIX = 49, 50, 51


def body(
    geometry,
    x_ref,
    adj_ref,
    kern_ref,
    bias_ref,
    gain_ref,
    shift_ref,
    scale_ref,
    out_ref,
    kgrad_ref,
    bgrad_ref,
    ggrad_ref,
    sgrad_ref,
    lgrad_ref,
    stage,
    own,
    mine,
    theirs,
    gathered,
    by_channel,
    weights,
    xbuf,
    xhalo,
    xpad,
    mixed,
    gbuf,
    gmix,
    ghalo,
    gpad,
    stats,
    kacc,
    terms,
    flat,
    pieces,
    got1,
    sum1,
    got2,
    sum2,
    got3,
    local_sem,
    p_send,
    p_recv,
    z_send,
    z_recv,
    x_send,
    x_recv,
    c_send,
    c_recv,
    ship_send,
    ship_recv,
    xh_send,
    xh_recv,
    gh_send,
    gh_recv,
    back_send,
    back_recv,
    r1_send,
    r1_recv,
    r2_send,
    r2_recv,
    r3_send,
    r3_recv,
):
    zs, xs_count, rows, cpd, chunks, height, width = geometry
    xcs = xs_count * CORES
    channels = chunks * LANES
    half = lax.axis_index("segment")
    other = 1 - half
    dp = lax.axis_index("dp")
    row = lax.axis_index("rows")
    z = dp // xcs
    xc = dp % xcs
    x = xc // CORES
    core = xc % CORES
    zz = z % rows

    def dp_of(z_at, xc_at):
        return z_at * xcs + xc_at

    def remote(src, dst, send, recv, **where):
        return pltpu.make_async_remote_copy(
            src_ref=src, dst_ref=dst, send_sem=send, recv_sem=recv, device_id=where, device_id_type=MESH
        )

    barrier = pltpu.get_barrier_semaphore()

    def greet(**where):
        pl.semaphore_signal(barrier, inc=1, device_id=where, device_id_type=MESH)

    own_x = pltpu.make_async_copy(x_ref.at[half], xbuf.at[half], local_sem.at[0])
    own_adj = pltpu.make_async_copy(adj_ref.at[half], gbuf.at[1], local_sem.at[1])
    own_x.start()
    own_adj.start()

    for k in range(1, zs):
        greet(dp=dp_of((z + k) % zs, xc))
    for k in range(1, xcs):
        greet(dp=dp_of(z, (xc + k) % xcs))
    for k in range(1, rows):
        greet(rows=(row + k) % rows)
    for k in range(rows):
        greet(segment=other, rows=(row + k) % rows)
    for k in range(zs):
        if k == 0:

            @pl.when(row != zz)
            def _():
                greet(rows=zz)
        else:
            greet(dp=dp_of((z + k) % zs, xc), rows=zz)

    stage[...] = jnp.zeros_like(stage)
    stage[BIAS : BIAS + 1, 0:cpd] = bias_ref[...].astype(F32)
    stage[GAIN : GAIN + 1, 0:cpd] = gain_ref[...].astype(F32)
    stage[SHIFT : SHIFT + 1, 0:cpd] = shift_ref[...].astype(F32)
    stage[SCALE : SCALE + 1, 0:cpd] = scale_ref[...].astype(F32)
    vectors = jnp.transpose(stage[...])[0:32]
    own[...] = jnp.zeros_like(own)
    own[0:cpd, 0:TAPS] = kern_ref[...].astype(F32)
    block = vectors + own[...]
    mine[...] = jnp.where(half == 1, pltpu.roll(block, 64, 1), block).astype(BF16)

    known = (zs - 1) + (xcs - 1) + (rows - 1) + rows + zs

    @pl.when(row != zz)
    def _():
        pl.semaphore_wait(barrier, known)

    @pl.when(row == zz)
    def _():
        pl.semaphore_wait(barrier, known - 1)

    swap = remote(mine, theirs, p_send.at[0], p_recv.at[0], segment=other)
    swap.start()

    ship = remote(x_ref.at[other], xbuf.at[half], ship_send.at[0], ship_recv.at[0], segment=other)
    shipped = remote(x_ref.at[other], xbuf.at[other], ship_send.at[0], ship_recv.at[0], segment=other)
    ship.start()

    def own_down():
        return remote(x_ref.at[half, height - 3 : height], xhalo.at[half, 0], xh_send.at[half, 0], xh_recv.at[half, 0], rows=(row + 1) % rows)

    def own_up():
        return remote(x_ref.at[half, 0:3], xhalo.at[half, 1], xh_send.at[half, 1], xh_recv.at[half, 1], rows=(row + rows - 1) % rows)

    def x_down(s):
        return remote(xbuf.at[s, height - 3 : height], xhalo.at[s, 0], xh_send.at[s, 0], xh_recv.at[s, 0], rows=(row + 1) % rows)

    def x_up(s):
        return remote(xbuf.at[s, 0:3], xhalo.at[s, 1], xh_send.at[s, 1], xh_recv.at[s, 1], rows=(row + rows - 1) % rows)

    def g_down(s):
        return remote(gmix.at[s, height - 3 : height], ghalo.at[s, 0], gh_send.at[s, 0], gh_recv.at[s, 0], rows=(row + 1) % rows)

    def g_up(s):
        return remote(gmix.at[s, 0:3], ghalo.at[s, 1], gh_send.at[s, 1], gh_recv.at[s, 1], rows=(row + rows - 1) % rows)

    @pl.when(row < rows - 1)
    def _():
        own_down().start()

    @pl.when(row > 0)
    def _():
        own_up().start()

    def clear(ch, carry):
        for s in range(2):
            for ref in (xpad, gpad):
                ref[s, ch, :, 0:OFF, :] = jnp.zeros((height + 6, OFF, LANES), F32)
                ref[s, ch, :, OFF + width : 2 * OFF + width, :] = jnp.zeros((height + 6, OFF, LANES), F32)
                ref[s, ch, 0:3, OFF : OFF + width, :] = jnp.zeros((3, width, LANES), F32)
                ref[s, ch, height + 3 : height + 6, OFF : OFF + width, :] = jnp.zeros((3, width, LANES), F32)
        return carry

    def lanes_of(ch):
        return pl.ds(pl.multiple_of(ch * LANES, LANES), LANES)

    def widen(s):
        def one(ch, carry):
            xpad[s, ch, 3 : 3 + height, OFF : OFF + width, :] = xbuf[s, :, :, lanes_of(ch)].astype(F32)
            return carry

        lax.fori_loop(0, chunks, one, 0)

    def z_copy(k):
        return remote(
            gathered.at[z, x, core],
            gathered.at[z, x, core],
            z_send.at[k - 1],
            z_recv.at[z],
            dp=dp_of((z + k) % zs, xc),
        )

    def z_arrival(k):
        src = (z + k) % zs
        return remote(
            gathered.at[src, x, core], gathered.at[src, x, core], z_send.at[k - 1], z_recv.at[src], dp=dp_of(src, xc)
        )

    def x_copy(k):
        return remote(
            gathered.at[:, x, core],
            gathered.at[:, x, core],
            x_send.at[k - 1],
            x_recv.at[x],
            dp=dp_of(z, ((x + k) % xs_count) * CORES + core),
        )

    def x_arrival(k):
        src = (x + k) % xs_count
        return remote(
            gathered.at[:, src, core],
            gathered.at[:, src, core],
            x_send.at[k - 1],
            x_recv.at[src],
            dp=dp_of(z, src * CORES + core),
        )

    def c_copy(k):
        src = (x + k) % xs_count
        return remote(
            gathered.at[:, src, core],
            gathered.at[:, src, core],
            c_send.at[k],
            c_recv.at[src],
            dp=dp_of(z, x * CORES + 1 - core),
        )

    def c_arrival(k):
        src = (x + k) % xs_count
        return remote(
            gathered.at[:, src, 1 - core],
            gathered.at[:, src, 1 - core],
            c_send.at[k],
            c_recv.at[src],
            dp=dp_of(z, x * CORES + 1 - core),
        )

    swap.wait_recv()
    gathered[z, x, core] = (mine[...].astype(F32) + theirs[...].astype(F32)).astype(BF16)
    for k in range(1, zs):
        z_copy(k).start()
    lax.fori_loop(0, chunks, clear, 0)
    for k in range(1, zs):
        z_arrival(k).wait_recv()
    for k in range(1, xs_count):
        x_copy(k).start()
    c_copy(0).start()
    own_x.wait()
    widen(half)
    for k in range(1, xs_count):
        x_arrival(k).wait_recv()
        c_copy(k).start()
    for k in range(xs_count):
        c_arrival(k).wait_recv()

    def place(d, carry):
        got = gathered[d // xcs, (d % xcs) // CORES, d % CORES].astype(F32)
        by_channel[pl.ds(pl.multiple_of(d * cpd, 8), cpd), :] = got[0:cpd]
        return carry

    lax.fori_loop(0, zs * xcs, place, 0)

    def turn(ch, carry):
        turned = jnp.transpose(by_channel[pl.ds(pl.multiple_of(ch * LANES, LANES), LANES), :])
        weights[0, ch] = turned[0:64]
        weights[1, ch] = turned[64:128]
        return carry

    lax.fori_loop(0, chunks, turn, 0)

    def put_halo(pad, halo, s, side, start):
        def one(ch, carry):
            pad[s, ch, start : start + 3, OFF : OFF + width, :] = halo[s, side, :, :, lanes_of(ch)].astype(F32)
            return carry

        lax.fori_loop(0, chunks, one, 0)

    def par(s, ch, which):
        return weights[s, ch, which : which + 1, :][None]

    inverse_count = 1.0 / channels

    def arrive(s):
        shipped.wait_recv()

        @pl.when(row < rows - 1)
        def _():
            x_down(s).start()

        @pl.when(row > 0)
        def _():
            x_up(s).start()

        widen(s)

    def forward(s):
        @pl.when(row > 0)
        def _():
            x_down(s).wait_recv()
            put_halo(xpad, xhalo, s, 0, 0)

        @pl.when(row < rows - 1)
        def _():
            x_up(s).wait_recv()
            put_halo(xpad, xhalo, s, 1, 3 + height)

        def conv(ch, total):
            acc = jnp.zeros((height, width, LANES), F32) + par(s, ch, BIAS)
            for c in range(7):
                shifted = xpad[s, ch, :, OFF - 3 + c : OFF - 3 + c + width, :]
                for r in range(7):
                    acc = acc + shifted[r : r + height] * par(s, ch, 7 * r + c)
            mixed[s, ch] = acc
            return total + acc

        total = lax.fori_loop(0, chunks, conv, jnp.zeros((height, width, LANES), F32))
        mean = jnp.sum(total, axis=-1, keepdims=True) * inverse_count
        stats[s, 0] = jnp.broadcast_to(mean, (height, width, LANES))
        mean = stats[s, 0]

        def spread(ch, total):
            centred = mixed[s, ch] - mean
            return total + centred * centred

        squares = lax.fori_loop(0, chunks, spread, jnp.zeros((height, width, LANES), F32))
        variance = jnp.sum(squares, axis=-1, keepdims=True) * inverse_count
        inverse = lax.rsqrt(variance + EPSILON)
        stats[s, 1] = jnp.broadcast_to(inverse, (height, width, LANES))

    def folded(value):
        flat_rows = jnp.sum(value, axis=0)
        total = flat_rows[0:8]
        for at in range(8, width, 8):
            total = total + flat_rows[at : at + 8]
        return total

    def norm_back(s):
        @pl.when(s == 1)
        def _():
            own_adj.wait()

        mean = stats[s, 0]
        inverse = stats[s, 1]

        def first(ch, sums):
            normed = (mixed[s, ch] - mean) * inverse
            mixed[s, ch] = normed
            upstream = gbuf[s, :, :, lanes_of(ch)].astype(F32)
            both = upstream * normed
            kacc[ch, SUM_G] = folded(upstream)
            kacc[ch, SUM_GN] = folded(both)
            factor = par(s, ch, SCALE) * par(s, ch, GAIN)
            return sums[0] + upstream * factor, sums[1] + both * factor

        zero = jnp.zeros((height, width, LANES), F32)
        plain, weighted = lax.fori_loop(0, chunks, first, (zero, zero))
        plain = jnp.sum(plain, axis=-1, keepdims=True) * inverse_count
        weighted = jnp.sum(weighted, axis=-1, keepdims=True) * inverse_count

        def second(ch, carry):
            upstream = gbuf[s, :, :, lanes_of(ch)].astype(F32)
            factor = par(s, ch, SCALE) * par(s, ch, GAIN)
            grad = inverse * (upstream * factor - plain - mixed[s, ch] * weighted)
            rounded = grad.astype(BF16)
            gmix[s, :, :, lanes_of(ch)] = rounded
            again = rounded.astype(F32)
            gpad[s, ch, 3 : 3 + height, OFF : OFF + width, :] = again
            kacc[ch, SUM_MIX] = folded(again)
            return carry

        lax.fori_loop(0, chunks, second, 0)

        @pl.when(row < rows - 1)
        def _():
            g_down(s).start()

        @pl.when(row > 0)
        def _():
            g_up(s).start()

    def keep_out(s):
        return pltpu.make_async_copy(gbuf.at[1 - s], out_ref.at[half], local_sem.at[2])

    def send_out(s):
        return remote(gbuf.at[1 - s], out_ref.at[half], back_send.at[0], back_recv.at[0], segment=other)

    def out_arrival():
        return remote(gbuf.at[0], out_ref.at[other], back_send.at[0], back_recv.at[0], segment=other)

    def adjoint(s):
        @pl.when(row > 0)
        def _():
            g_down(s).wait_recv()
            put_halo(gpad, ghalo, s, 0, 0)

        @pl.when(row < rows - 1)
        def _():
            g_up(s).wait_recv()
            put_halo(gpad, ghalo, s, 1, 3 + height)

        def conv(ch, carry):
            acc = gbuf[s, :, :, lanes_of(ch)].astype(F32)
            for c in range(7):
                shifted = gpad[s, ch, :, OFF + 3 - c : OFF + 3 - c + width, :]
                for r in range(7):
                    acc = acc + shifted[6 - r : 6 - r + height] * par(s, ch, 7 * r + c)
            gbuf[1 - s, :, :, lanes_of(ch)] = acc.astype(BF16)
            return carry

        lax.fori_loop(0, chunks, conv, 0)

        @pl.when(s == half)
        def _():
            keep_out(s).start()

        @pl.when(s != half)
        def _():
            send_out(s).start()

    def r1_copy(s, k):
        to = (xc + k) % xcs
        return remote(pieces.at[s, :, to], got1.at[s, xc], r1_send.at[s, k - 1], r1_recv.at[s, xc], dp=dp_of(z, to))

    def r1_arrival(s, k):
        src = (xc + k) % xcs
        return remote(pieces.at[s, :, src], got1.at[s, src], r1_send.at[s, k - 1], r1_recv.at[s, src], dp=dp_of(z, src))

    def taps(s):
        def one(ch, carry):
            grad = gpad[s, ch, 3 : 3 + height, OFF : OFF + width, :]
            for c in range(7):
                shifted = xpad[s, ch, :, OFF - 3 + c : OFF - 3 + c + width, :]
                for r in range(7):
                    kacc[ch, 7 * r + c] = folded(shifted[r : r + height] * grad)
            return carry

        lax.fori_loop(0, chunks, one, 0)

        def total(ch, carry):
            terms[ch] = jnp.zeros((64, LANES), F32)
            for t in range(TAPS + 3):
                terms[ch, t : t + 1, :] = jnp.sum(kacc[ch, t], axis=0, keepdims=True)
            return carry

        lax.fori_loop(0, chunks, total, 0)
        middle = chunks // 2

        def turn_back(ch, carry):
            joined = jnp.concatenate([terms[ch], terms[middle + ch]], axis=0)
            flat[pl.ds(pl.multiple_of(ch * LANES, LANES), LANES), :] = jnp.transpose(joined)
            return carry

        lax.fori_loop(0, middle, turn_back, 0)

        def cut(d, carry):
            pieces[s, d // xcs, d % xcs] = flat[pl.ds(pl.multiple_of(d * cpd, 8), cpd), :]
            return carry

        lax.fori_loop(0, rows * xcs, cut, 0)
        for k in range(1, xcs):
            r1_copy(s, k).start()

    ARRIVE, FORWARD, NORM, TAPS_OF, ADJOINT = range(5)
    lower = ((ARRIVE, 1), (FORWARD, 0), (FORWARD, 1), (NORM, 1), (TAPS_OF, 1), (ADJOINT, 1), (NORM, 0), (TAPS_OF, 0), (ADJOINT, 0))
    upper = ((FORWARD, 1), (NORM, 1), (ARRIVE, 0), (TAPS_OF, 1), (FORWARD, 0), (ADJOINT, 1), (NORM, 0), (TAPS_OF, 0), (ADJOINT, 0))

    def digits(order, which, base):
        return sum(entry[which] * base**at for at, entry in enumerate(order))

    kinds = digits(lower, 0, 8) + half * (digits(upper, 0, 8) - digits(lower, 0, 8))
    slots = digits(lower, 1, 2) + half * (digits(upper, 1, 2) - digits(lower, 1, 2))

    def step(at, carry):
        kinds_left, slots_left = carry
        kind = kinds_left % 8
        s = slots_left % 2
        for number, act in ((ARRIVE, arrive), (FORWARD, forward), (NORM, norm_back), (TAPS_OF, taps), (ADJOINT, adjoint)):

            @pl.when(kind == number)
            def _():
                act(s)

        return kinds_left // 8, slots_left // 2

    lax.fori_loop(0, len(lower), step, (kinds, slots))

    def r2_copy(s, k):
        to = (row + k) % rows
        return remote(
            sum1.at[s, to], got2.at[half, row], r2_send.at[s, k], r2_recv.at[half, row], segment=s, rows=to
        )

    def r2_arrival(k, from_half):
        src = (row + k) % rows
        return remote(
            sum1.at[0, src], got2.at[from_half, src], r2_send.at[0, k], r2_recv.at[from_half, src], segment=other, rows=src
        )

    for s in (1, 0):
        for k in range(1, xcs):
            r1_arrival(s, k).wait_recv()
        got1[s, xc] = pieces[s, :, xc]
        acc = got1[s, 0]
        for k in range(1, xcs):
            acc = acc + got1[s, k]
        sum1[s] = acc

        @pl.when(half == s)
        def _():
            got2[half, row] = sum1[s, row]

        @pl.when(half != s)
        def _():
            r2_copy(s, 0).start()

        for k in range(1, rows):
            r2_copy(s, k).start()

    for k in range(rows):
        if k > 0:
            r2_arrival(k, half).wait_recv()
        r2_arrival(k, other).wait_recv()
    acc = got2[0, 0] + got2[1, 0]
    for k in range(1, rows):
        acc = acc + (got2[0, k] + got2[1, k])
    sum2[...] = acc

    def r3_copy(part, k):
        to_z = part * rows + row
        return remote(sum2, got3.at[z], r3_send.at[part, k], r3_recv.at[z], dp=dp_of(to_z, xc), rows=(row + k) % rows)

    def r3_arrival(k):
        src = (z + k) % zs
        return remote(sum2, got3.at[src], r3_send.at[0, 0], r3_recv.at[src], dp=dp_of(src, xc), rows=zz)

    for part in range(2):
        for k in range(rows):
            if k == 0:

                @pl.when(z != part * rows + row)
                def _():
                    r3_copy(part, 0).start()
            else:
                r3_copy(part, k).start()

    @pl.when(row == zz)
    def _():
        got3[z] = sum2[...]

    @pl.when(row != zz)
    def _():
        r3_arrival(0).wait_recv()

    for k in range(1, zs):
        r3_arrival(k).wait_recv()
    acc = got3[0]
    for k in range(1, zs):
        acc = acc + got3[k]
    scale_by = 1.0 / (2 * zs * xcs)
    acc = jnp.where(z // rows == 1, pltpu.roll(acc, 64, 1), acc) * scale_by
    kgrad_ref[...] = acc[:, 0:TAPS]
    stage[...] = jnp.zeros_like(stage)
    stage[0:cpd, :] = acc
    turned = jnp.transpose(stage[...])
    sum_g = turned[SUM_G : SUM_G + 1, 0:cpd]
    sum_gn = turned[SUM_GN : SUM_GN + 1, 0:cpd]
    bgrad_ref[...] = turned[SUM_MIX : SUM_MIX + 1, 0:cpd]
    own_scale = scale_ref[...].astype(F32)
    ggrad_ref[...] = own_scale * sum_gn
    sgrad_ref[...] = own_scale * sum_g
    lgrad_ref[...] = gain_ref[...].astype(F32) * sum_gn + shift_ref[...].astype(F32) * sum_g

    swap.wait_send()
    ship.wait_send()
    for k in range(1, zs):
        z_copy(k).wait_send()
    for k in range(1, xs_count):
        x_copy(k).wait_send()
    for k in range(xs_count):
        c_copy(k).wait_send()
    for s in range(2):

        @pl.when(row < rows - 1)
        def _():
            x_down(s).wait_send()
            g_down(s).wait_send()

        @pl.when(row > 0)
        def _():
            x_up(s).wait_send()
            g_up(s).wait_send()

        for k in range(1, xcs):
            r1_copy(s, k).wait_send()
        for k in range(1, rows):
            r2_copy(s, k).wait_send()

        @pl.when(half != s)
        def _():
            r2_copy(s, 0).wait_send()

    for part in range(2):
        for k in range(rows):
            if k == 0:

                @pl.when(z != part * rows + row)
                def _():
                    r3_copy(part, 0).wait_send()
            else:
                r3_copy(part, k).wait_send()
    keep_out(0).wait()
    send_out(0).wait_send()
    out_arrival().wait_recv()


def local(xs_count, section_input, adjoint_in, kernel, conv_bias, ln_gain, ln_shift, layer_scale):
    _, micros, images, height, width, channels = section_input.shape
    cpd = kernel.shape[3]
    rows = lax.axis_size("rows")
    zs = lax.axis_size("dp") // (xs_count * CORES)
    xcs = xs_count * CORES
    chunks = channels // LANES
    vmem = pl.BlockSpec(memory_space=pltpu.VMEM)
    hbm = pl.BlockSpec(memory_space=pltpu.HBM)
    vec = jax.ShapeDtypeStruct((1, cpd), F32)
    dma = pltpu.SemaphoreType.DMA
    scratch = [
        pltpu.VMEM((LANES, LANES), F32),
        pltpu.VMEM((32, LANES), F32),
        pltpu.VMEM((32, LANES), BF16),
        pltpu.VMEM((32, LANES), BF16),
        pltpu.VMEM((zs, xs_count, CORES, 32, LANES), BF16),
        pltpu.VMEM((channels, LANES), F32),
        pltpu.VMEM((2, chunks, 64, LANES), F32),
        pltpu.VMEM((2, height, width, channels), BF16),
        pltpu.VMEM((2, 2, 3, width, channels), BF16),
        pltpu.VMEM((2, chunks, height + 6, width + 2 * OFF, LANES), F32),
        pltpu.VMEM((2, chunks, height, width, LANES), F32),
        pltpu.VMEM((2, height, width, channels), BF16),
        pltpu.VMEM((2, height, width, channels), BF16),
        pltpu.VMEM((2, 2, 3, width, channels), BF16),
        pltpu.VMEM((2, chunks, height + 6, width + 2 * OFF, LANES), F32),
        pltpu.VMEM((2, 2, height, width, LANES), F32),
        pltpu.VMEM((chunks, TAPS + 3, 8, LANES), F32),
        pltpu.VMEM((chunks, 64, LANES), F32),
        pltpu.VMEM((channels // 2, LANES), F32),
        pltpu.VMEM((2, rows, xcs, cpd, LANES), F32),
        pltpu.VMEM((2, xcs, rows, cpd, LANES), F32),
        pltpu.VMEM((2, rows, cpd, LANES), F32),
        pltpu.VMEM((2, rows, cpd, LANES), F32),
        pltpu.VMEM((cpd, LANES), F32),
        pltpu.VMEM((zs, cpd, LANES), F32),
        dma((3,)),
        dma((1,)),
        dma((1,)),
        dma((zs,)),
        dma((zs,)),
        dma((xs_count,)),
        dma((xs_count,)),
        dma((xs_count,)),
        dma((xs_count,)),
        dma((1,)),
        dma((1,)),
        dma((2, 2)),
        dma((2, 2)),
        dma((2, 2)),
        dma((2, 2)),
        dma((1,)),
        dma((1,)),
        dma((2, xcs)),
        dma((2, xcs)),
        dma((2, rows)),
        dma((2, rows)),
        dma((2, rows)),
        dma((zs,)),
    ]
    found = pl.pallas_call(
        functools.partial(body, (zs, xs_count, rows, cpd, chunks, height, width)),
        out_shape=(
            jax.ShapeDtypeStruct((micros, height, width, channels), BF16),
            jax.ShapeDtypeStruct((cpd, TAPS), F32),
            vec,
            vec,
            vec,
            vec,
        ),
        in_specs=[hbm, hbm] + [vmem] * 5,
        out_specs=(vmem,) * 6,
        scratch_shapes=scratch,
        compiler_params=pltpu.CompilerParams(
            collective_id=0, has_side_effects=True, vmem_limit_bytes=48 * 1024 * 1024
        ),
    )(
        section_input.reshape(micros, height, width, channels),
        adjoint_in.reshape(micros, height, width, channels),
        kernel.reshape(TAPS, cpd).T,
        conv_bias.reshape(1, cpd),
        ln_gain.reshape(1, cpd),
        ln_shift.reshape(1, cpd),
        layer_scale.reshape(1, cpd),
    )
    adjoint, kgrad, bgrad, ggrad, sgrad, lgrad = found
    return (
        adjoint.reshape(section_input.shape),
        kgrad.T.reshape(kernel.shape),
        bgrad.reshape(conv_bias.shape),
        ggrad.reshape(conv_bias.shape),
        sgrad.reshape(conv_bias.shape),
        lgrad.reshape(conv_bias.shape),
    )


def solution(mesh, xs_count=XS):
    placed = (
        P("segment", None, "dp", "rows", None, None),
        P(None, "dp", "rows", None, None),
        P("segment", None, None, "dp"),
        P("segment", None, "dp"),
        P("segment", None, "dp"),
        P("segment", None, "dp"),
        P("segment", None, "dp"),
    )
    return jax.shard_map(
        functools.partial(local, xs_count),
        mesh=mesh,
        in_specs=placed,
        out_specs=(placed[0],) + (placed[2],) + (placed[3],) * 4,
        check_vma=False,
    )
```

time: 103 us -> 89.6 us (0.87)
  Pallas kernels: 96.2 us -> 82.5 us
    pallas_call x1, Pallas kernels: 96.2 us -> 82.5 us  [local(): pl.pallas_call(functools.partial(body, (zs, xs_count, rows, cpd, chunks,...]
where the time goes in v2:
time: 89.6 us; the launch traced here: 89.4 us
  Pallas kernels  82.5 us (92%)
  local copies, waits for them, and re-layouts  6.16 us (7%)
    pallas_call x1, Pallas kernels, local(): pl.pallas_call(functools.partial(body, (zs, xs_count, rows, cpd, chunks,...  82.5 us
    unnamed x20, local copies, waits for them, and re-layouts  6.16 us

profile of v2, /device:TPU:8, one launch (start us, length us, event | category | flops | bytes accessed | tf_op | source)
XLA Modules:
  0.0 89.4 jit_solution(11459263277648583562)
XLA Ops:
  0.6 0.0 copy-start.2
  0.6 0.0 copy-start.6
  0.7 0.0 copy-start.3
  0.7 0.0 copy-start.4
  0.7 0.0 copy-start.5
  0.7 0.6 copy-done.2
  1.3 0.0 copy-done.6
  1.3 0.0 copy-done.3
  1.3 0.0 copy-done.4
  1.3 0.0 copy-done.5
  1.4 0.0 copy-start
  1.4 1.0 %copy-done = bf16[1,2,1,5,16,1536]{5,4,3,2,1,0:T(8,128)(2,1)S(1)} copy-done((bf16[1,2,1,5,16,1536]{5,4,3,2,1,0:T(8,128)(2,1)S(1)}, bf16[1,2,1,5,16,1536]{5,4,3,2,1,0:T(8,128)(2,1)}, u32[]{:S(2)}) %copy-start) | copy-done | bytes 491544
  2.4 0.0 copy-start.1
  2.4 1.0 %copy-done.1 = bf16[2,1,5,16,1536]{4,3,2,1,0:T(8,128)(2,1)S(1)} copy-done((bf16[2,1,5,16,1536]{4,3,2,1,0:T(8,128)(2,1)S(1)}, bf16[2,1,5,16,1536]{4,3,2,1,0:T(8,128)(2,1)}, u32[]{:S(2)}) %copy-start.1) | copy-done | bytes 491544
  3.4 82.5 %shard_map.118 = (bf16[2,5,16,1536]{3,2,1,0:T(8,128)(2,1)S(1)}, f32[24,49]{1,0:T(8,128)S(1)}, f32[1,24]{1,0:T(1,128)S(1)}, f32[1,24]{1,0:T(1,128)S(1)}, f32[1,24]{1,0:T(1,128)S(1)}, /*index=5*/f32[1,24]{1,0:T(1,128)S(1)}) custom-call(bf16[2,5,16,1536]{3,2,1,0:T(8,128)(2,1)S(1)} %bitcast.19, bf16[2,5,16,1536]{3,2,1,0:T(8,128)(2,1)S(1)} %bitcast.20, ...), custom_call_target="tpu_custom_call" | custom-call | tf_op jit(solution)/shard_map/pallas_call | solution.py:701
  86.0 0.8 copy.20
  86.7 0.6 copy.21
  87.3 0.5 copy.22
  87.9 0.5 copy.23
  88.4 0.5 copy.24
  88.9 0.5 copy.25
Async XLA Ops:
  0.6 0.7 copy-start.2
  0.6 0.7 copy-start.6
  0.7 0.7 copy-start.3
  0.7 0.7 copy-start.4
  0.7 0.7 copy-start.5
  1.4 1.0 %copy-start = (bf16[1,2,1,5,16,1536]{5,4,3,2,1,0:T(8,128)(2,1)S(1)}, bf16[1,2,1,5,16,1536]{5,4,3,2,1,0:T(8,128)(2,1)}, u32[]{:S(2)}) copy-start(bf16[1,2,1,5,16,1536]{5,4,3,2,1,0:T(8,128)(2,1)} %param.7) | copy-start | bytes 1474564
  2.4 1.0 %copy-start.1 = (bf16[2,1,5,16,1536]{4,3,2,1,0:T(8,128)(2,1)S(1)}, bf16[2,1,5,16,1536]{4,3,2,1,0:T(8,128)(2,1)}, u32[]{:S(2)}) copy-start(bf16[2,1,5,16,1536]{4,3,2,1,0:T(8,128)(2,1)} %param.8) | copy-start | bytes 1474564

commit v3 on v2

--- a/solution.py
+++ b/solution.py
@@ -30,15 +30,9 @@
     shift_ref,
     scale_ref,
     out_ref,
-    kgrad_ref,
-    bgrad_ref,
-    ggrad_ref,
-    sgrad_ref,
-    lgrad_ref,
+    sums_ref,
     stage,
     own,
-    mine,
-    theirs,
     gathered,
     by_channel,
     weights,
@@ -140,8 +134,9 @@
     vectors = jnp.transpose(stage[...])[0:32]
     own[...] = jnp.zeros_like(own)
     own[0:cpd, 0:TAPS] = kern_ref[...].astype(F32)
-    block = vectors + own[...]
-    mine[...] = jnp.where(half == 1, pltpu.roll(block, 64, 1), block).astype(BF16)
+    own[...] = own[...] + vectors
+    mid = cpd // 2
+    gathered[half, z, x, core] = (own[0:16] + pltpu.roll(own[mid : mid + 16], 64, 1)).astype(BF16)
 
     known = (zs - 1) + (xcs - 1) + (rows - 1) + rows + zs
 
@@ -153,7 +148,9 @@
     def _():
         pl.semaphore_wait(barrier, known - 1)
 
-    swap = remote(mine, theirs, p_send.at[0], p_recv.at[0], segment=other)
+    mine = gathered.at[half, z, x, core]
+    swap = remote(mine, mine, p_send.at[0], p_recv.at[0], segment=other)
+    swapped = remote(mine, gathered.at[other, z, x, core], p_send.at[0], p_recv.at[0], segment=other)
     swap.start()
 
     ship = remote(x_ref.at[other], xbuf.at[half], ship_send.at[0], ship_recv.at[0], segment=other)
@@ -205,92 +202,82 @@
 
         lax.fori_loop(0, chunks, one, 0)
 
-    def z_copy(k):
-        return remote(
-            gathered.at[z, x, core],
-            gathered.at[z, x, core],
-            z_send.at[k - 1],
-            z_recv.at[z],
-            dp=dp_of((z + k) % zs, xc),
-        )
-
-    def z_arrival(k):
+    def z_copy(s, k):
+        block = gathered.at[s, z, x, core]
+        return remote(block, block, z_send.at[s, k - 1], z_recv.at[s, z], dp=dp_of((z + k) % zs, xc))
+
+    def z_arrival(s, k):
         src = (z + k) % zs
-        return remote(
-            gathered.at[src, x, core], gathered.at[src, x, core], z_send.at[k - 1], z_recv.at[src], dp=dp_of(src, xc)
-        )
-
-    def x_copy(k):
-        return remote(
-            gathered.at[:, x, core],
-            gathered.at[:, x, core],
-            x_send.at[k - 1],
-            x_recv.at[x],
-            dp=dp_of(z, ((x + k) % xs_count) * CORES + core),
-        )
-
-    def x_arrival(k):
+        block = gathered.at[s, src, x, core]
+        return remote(block, block, z_send.at[s, k - 1], z_recv.at[s, src], dp=dp_of(src, xc))
+
+    def x_copy(s, k):
+        to = (x + k) % xs_count
+        block = gathered.at[s, :, x, core]
+        return remote(block, block, x_send.at[s, k - 1], x_recv.at[s, x], dp=dp_of(z, to * CORES + core))
+
+    def x_arrival(s, k):
         src = (x + k) % xs_count
-        return remote(
-            gathered.at[:, src, core],
-            gathered.at[:, src, core],
-            x_send.at[k - 1],
-            x_recv.at[src],
-            dp=dp_of(z, src * CORES + core),
-        )
-
-    def c_copy(k):
+        block = gathered.at[s, :, src, core]
+        return remote(block, block, x_send.at[s, k - 1], x_recv.at[s, src], dp=dp_of(z, src * CORES + core))
+
+    def c_copy(s, k):
         src = (x + k) % xs_count
-        return remote(
-            gathered.at[:, src, core],
-            gathered.at[:, src, core],
-            c_send.at[k],
-            c_recv.at[src],
-            dp=dp_of(z, x * CORES + 1 - core),
-        )
-
-    def c_arrival(k):
+        block = gathered.at[s, :, src, core]
+        return remote(block, block, c_send.at[s, k], c_recv.at[s, src], dp=dp_of(z, x * CORES + 1 - core))
+
+    def c_arrival(s, k):
         src = (x + k) % xs_count
-        return remote(
-            gathered.at[:, src, 1 - core],
-            gathered.at[:, src, 1 - core],
-            c_send.at[k],
-            c_recv.at[src],
-            dp=dp_of(z, x * CORES + 1 - core),
-        )
-
-    swap.wait_recv()
-    gathered[z, x, core] = (mine[...].astype(F32) + theirs[...].astype(F32)).astype(BF16)
-    for k in range(1, zs):
-        z_copy(k).start()
+        block = gathered.at[s, :, src, 1 - core]
+        return remote(block, block, c_send.at[s, k], c_recv.at[s, src], dp=dp_of(z, x * CORES + 1 - core))
+
+    def over_z(s):
+        for k in range(1, zs):
+            z_copy(s, k).start()
+
+    def over_x(s):
+        for k in range(1, zs):
+            z_arrival(s, k).wait_recv()
+        for k in range(1, xs_count):
+            x_copy(s, k).start()
+        c_copy(s, 0).start()
+
+    def over_core(s):
+        for k in range(1, xs_count):
+            x_arrival(s, k).wait_recv()
+            c_copy(s, k).start()
+
+    def settle(s):
+        for k in range(xs_count):
+            c_arrival(s, k).wait_recv()
+
+        def place(at, carry):
+            got = gathered[s, at].astype(F32)
+            turned = pltpu.roll(got, 64, 3)
+            for d in range(xcs):
+                by_channel[at, d * cpd : d * cpd + mid, :] = got[d // CORES, d % CORES, 0:mid]
+                by_channel[at, d * cpd + mid : (d + 1) * cpd, :] = turned[d // CORES, d % CORES, 0:mid]
+            return carry
+
+        lax.fori_loop(0, zs, place, 0)
+        span = xcs * cpd
+        for ch in range(chunks):
+            first, parts = ch * LANES, []
+            while first < (ch + 1) * LANES:
+                last = min((first // span + 1) * span, (ch + 1) * LANES)
+                parts.append(by_channel[first // span, first % span : first % span + last - first, :])
+                first = last
+            weights[s, ch] = jnp.transpose(jnp.concatenate(parts, axis=0) if len(parts) > 1 else parts[0])[0:64]
+
+    over_z(half)
     lax.fori_loop(0, chunks, clear, 0)
-    for k in range(1, zs):
-        z_arrival(k).wait_recv()
-    for k in range(1, xs_count):
-        x_copy(k).start()
-    c_copy(0).start()
+    over_x(half)
     own_x.wait()
     widen(half)
-    for k in range(1, xs_count):
-        x_arrival(k).wait_recv()
-        c_copy(k).start()
-    for k in range(xs_count):
-        c_arrival(k).wait_recv()
-
-    def place(d, carry):
-        got = gathered[d // xcs, (d % xcs) // CORES, d % CORES].astype(F32)
-        by_channel[pl.ds(pl.multiple_of(d * cpd, 8), cpd), :] = got[0:cpd]
-        return carry
-
-    lax.fori_loop(0, zs * xcs, place, 0)
-
-    def turn(ch, carry):
-        turned = jnp.transpose(by_channel[pl.ds(pl.multiple_of(ch * LANES, LANES), LANES), :])
-        weights[0, ch] = turned[0:64]
-        weights[1, ch] = turned[64:128]
-        return carry
-
-    lax.fori_loop(0, chunks, turn, 0)
+    over_core(half)
+    swapped.wait_recv()
+    over_z(other)
+    settle(half)
 
     def put_halo(pad, halo, s, side, start):
         def one(ch, carry):
@@ -350,6 +337,10 @@
         variance = jnp.sum(squares, axis=-1, keepdims=True) * inverse_count
         inverse = lax.rsqrt(variance + EPSILON)
         stats[s, 1] = jnp.broadcast_to(inverse, (height, width, LANES))
+
+        @pl.when(s == half)
+        def _():
+            over_x(other)
 
     def folded(value):
         flat_rows = jnp.sum(value, axis=0)
@@ -469,44 +460,37 @@
         lax.fori_loop(0, chunks, total, 0)
         middle = chunks // 2
 
-        def turn_back(ch, carry):
+        for ch in range(middle):
             joined = jnp.concatenate([terms[ch], terms[middle + ch]], axis=0)
-            flat[pl.ds(pl.multiple_of(ch * LANES, LANES), LANES), :] = jnp.transpose(joined)
-            return carry
-
-        lax.fori_loop(0, middle, turn_back, 0)
-
-        def cut(d, carry):
-            pieces[s, d // xcs, d % xcs] = flat[pl.ds(pl.multiple_of(d * cpd, 8), cpd), :]
-            return carry
-
-        lax.fori_loop(0, rows * xcs, cut, 0)
+            flat[ch * LANES : (ch + 1) * LANES, :] = jnp.transpose(joined)
+        for d in range(rows * xcs):
+            pieces[s, d // xcs, d % xcs] = flat[d * cpd : (d + 1) * cpd, :]
         for k in range(1, xcs):
             r1_copy(s, k).start()
 
-    ARRIVE, FORWARD, NORM, TAPS_OF, ADJOINT = range(5)
-    lower = ((ARRIVE, 1), (FORWARD, 0), (FORWARD, 1), (NORM, 1), (TAPS_OF, 1), (ADJOINT, 1), (NORM, 0), (TAPS_OF, 0), (ADJOINT, 0))
-    upper = ((FORWARD, 1), (NORM, 1), (ARRIVE, 0), (TAPS_OF, 1), (FORWARD, 0), (ADJOINT, 1), (NORM, 0), (TAPS_OF, 0), (ADJOINT, 0))
-
-    def digits(order, which, base):
-        return sum(entry[which] * base**at for at, entry in enumerate(order))
-
-    kinds = digits(lower, 0, 8) + half * (digits(upper, 0, 8) - digits(lower, 0, 8))
-    slots = digits(lower, 1, 2) + half * (digits(upper, 1, 2) - digits(lower, 1, 2))
-
-    def step(at, carry):
-        kinds_left, slots_left = carry
-        kind = kinds_left % 8
-        s = slots_left % 2
-        for number, act in ((ARRIVE, arrive), (FORWARD, forward), (NORM, norm_back), (TAPS_OF, taps), (ADJOINT, adjoint)):
-
-            @pl.when(kind == number)
+    ARRIVE, FORWARD, NORM, TAPS_OF, ADJOINT, OVER_CORE, SETTLE = range(7)
+    lower = ((FORWARD, 0), (ARRIVE, 1), (OVER_CORE, 1), (SETTLE, 1), (FORWARD, 1), (NORM, 1), (TAPS_OF, 1))
+    upper = ((FORWARD, 1), (NORM, 1), (OVER_CORE, 0), (ARRIVE, 0), (TAPS_OF, 1), (SETTLE, 0), (FORWARD, 0))
+    common = ((ADJOINT, 1), (NORM, 0), (TAPS_OF, 0), (ADJOINT, 0))
+    acts = (arrive, forward, norm_back, taps, adjoint, over_core, settle)
+
+    def digits(order):
+        return sum((2 * kind + s) * 16**at for at, (kind, s) in enumerate(order))
+
+    codes = digits(lower) + half * (digits(upper) - digits(lower))
+
+    def step(at, left):
+        code = left % 16
+        s = code % 2
+        for number, act in enumerate(acts):
+
+            @pl.when(code // 2 == number)
             def _():
                 act(s)
 
-        return kinds_left // 8, slots_left // 2
-
-    lax.fori_loop(0, len(lower), step, (kinds, slots))
+        return jnp.where(at == len(lower) - 1, digits(common), left // 16)
+
+    lax.fori_loop(0, len(lower) + len(common), step, codes)
 
     def r2_copy(s, k):
         to = (row + k) % rows
@@ -581,10 +565,64 @@
     for k in range(1, zs):
         acc = acc + got3[k]
     scale_by = 1.0 / (2 * zs * xcs)
-    acc = jnp.where(z // rows == 1, pltpu.roll(acc, 64, 1), acc) * scale_by
-    kgrad_ref[...] = acc[:, 0:TAPS]
+    sums_ref[...] = jnp.where(z // rows == 1, pltpu.roll(acc, 64, 1), acc) * scale_by
+
+    swap.wait_send()
+    ship.wait_send()
+    for s in range(2):
+        for k in range(1, zs):
+            z_copy(s, k).wait_send()
+        for k in range(1, xs_count):
+            x_copy(s, k).wait_send()
+        for k in range(xs_count):
+            c_copy(s, k).wait_send()
+
+        @pl.when(row < rows - 1)
+        def _():
+            x_down(s).wait_send()
+            g_down(s).wait_send()
+
+        @pl.when(row > 0)
+        def _():
+            x_up(s).wait_send()
+            g_up(s).wait_send()
+
+        for k in range(1, xcs):
+            r1_copy(s, k).wait_send()
+        for k in range(1, rows):
+            r2_copy(s, k).wait_send()
+
+        @pl.when(half != s)
+        def _():
+            r2_copy(s, 0).wait_send()
+
+    for part in range(2):
+        for k in range(rows):
+            if k == 0:
+
+                @pl.when(z != part * rows + row)
+                def _():
+                    r3_copy(part, 0).wait_send()
+            else:
+                r3_copy(part, k).wait_send()
+    keep_out(0).wait()
+    send_out(0).wait_send()
+    out_arrival().wait_recv()
+
+
+def finish(whole_ref, sums_ref, gain_ref, shift_ref, scale_ref, out_ref, kgrad_ref, bgrad_ref, ggrad_ref, sgrad_ref, lgrad_ref, held, stage, sem):
+    count = held.shape[0]
+    fetch = [pltpu.make_async_copy(whole_ref.at[m], held.at[m], sem.at[0, m]) for m in range(count)]
+    place = [pltpu.make_async_copy(held.at[m], out_ref.at[m], sem.at[1, m]) for m in range(count)]
+    for m in range(count):
+        fetch[m].start()
+    for m in range(count):
+        fetch[m].wait()
+        place[m].start()
+    cpd = sums_ref.shape[0]
+    kgrad_ref[...] = sums_ref[:, 0:TAPS]
     stage[...] = jnp.zeros_like(stage)
-    stage[0:cpd, :] = acc
+    stage[0:cpd, :] = sums_ref[...]
     turned = jnp.transpose(stage[...])
     sum_g = turned[SUM_G : SUM_G + 1, 0:cpd]
     sum_gn = turned[SUM_GN : SUM_GN + 1, 0:cpd]
@@ -593,48 +631,8 @@
     ggrad_ref[...] = own_scale * sum_gn
     sgrad_ref[...] = own_scale * sum_g
     lgrad_ref[...] = gain_ref[...].astype(F32) * sum_gn + shift_ref[...].astype(F32) * sum_g
-
-    swap.wait_send()
-    ship.wait_send()
-    for k in range(1, zs):
-        z_copy(k).wait_send()
-    for k in range(1, xs_count):
-        x_copy(k).wait_send()
-    for k in range(xs_count):
-        c_copy(k).wait_send()
-    for s in range(2):
-
-        @pl.when(row < rows - 1)
-        def _():
-            x_down(s).wait_send()
-            g_down(s).wait_send()
-
-        @pl.when(row > 0)
-        def _():
-            x_up(s).wait_send()
-            g_up(s).wait_send()
-
-        for k in range(1, xcs):
-            r1_copy(s, k).wait_send()
-        for k in range(1, rows):
-            r2_copy(s, k).wait_send()
-
-        @pl.when(half != s)
-        def _():
-            r2_copy(s, 0).wait_send()
-
-    for part in range(2):
-        for k in range(rows):
-            if k == 0:
-
-                @pl.when(z != part * rows + row)
-                def _():
-                    r3_copy(part, 0).wait_send()
-            else:
-                r3_copy(part, k).wait_send()
-    keep_out(0).wait()
-    send_out(0).wait_send()
-    out_arrival().wait_recv()
+    for m in range(count):
+        place[m].wait()
 
 
 def local(xs_count, section_input, adjoint_in, kernel, conv_bias, ln_gain, ln_shift, layer_scale):
@@ -651,10 +649,8 @@
     scratch = [
         pltpu.VMEM((LANES, LANES), F32),
         pltpu.VMEM((32, LANES), F32),
-        pltpu.VMEM((32, LANES), BF16),
-        pltpu.VMEM((32, LANES), BF16),
-        pltpu.VMEM((zs, xs_count, CORES, 32, LANES), BF16),
-        pltpu.VMEM((channels, LANES), F32),
+        pltpu.VMEM((2, zs, xs_count, CORES, 16, LANES), BF16),
+        pltpu.VMEM((zs, xcs * cpd, LANES), F32),
         pltpu.VMEM((2, chunks, 64, LANES), F32),
         pltpu.VMEM((2, height, width, channels), BF16),
         pltpu.VMEM((2, 2, 3, width, channels), BF16),
@@ -677,12 +673,12 @@
         dma((3,)),
         dma((1,)),
         dma((1,)),
-        dma((zs,)),
-        dma((zs,)),
-        dma((xs_count,)),
-        dma((xs_count,)),
-        dma((xs_count,)),
-        dma((xs_count,)),
+        dma((2, zs)),
+        dma((2, zs)),
+        dma((2, xs_count)),
+        dma((2, xs_count)),
+        dma((2, xs_count)),
+        dma((2, xs_count)),
         dma((1,)),
         dma((1,)),
         dma((2, 2)),
@@ -698,8 +694,27 @@
         dma((2, rows)),
         dma((zs,)),
     ]
-    found = pl.pallas_call(
+    vectors = [vector.reshape(1, cpd) for vector in (conv_bias, ln_gain, ln_shift, layer_scale)]
+    whole, sums = pl.pallas_call(
         functools.partial(body, (zs, xs_count, rows, cpd, chunks, height, width)),
+        out_shape=(
+            jax.ShapeDtypeStruct((micros, height, width, channels), BF16),
+            jax.ShapeDtypeStruct((cpd, LANES), F32),
+        ),
+        in_specs=[hbm, hbm] + [vmem] * 5,
+        out_specs=(hbm, vmem),
+        scratch_shapes=scratch,
+        compiler_params=pltpu.CompilerParams(
+            collective_id=0, has_side_effects=True, vmem_limit_bytes=60 * 1024 * 1024
+        ),
+    )(
+        section_input.reshape(micros, height, width, channels),
+        adjoint_in.reshape(micros, height, width, channels),
+        kernel.reshape(TAPS, cpd).T,
+        *vectors,
+    )
+    adjoint, kgrad, bgrad, ggrad, sgrad, lgrad = pl.pallas_call(
+        finish,
         out_shape=(
             jax.ShapeDtypeStruct((micros, height, width, channels), BF16),
             jax.ShapeDtypeStruct((cpd, TAPS), F32),
@@ -708,22 +723,15 @@
             vec,
             vec,
         ),
-        in_specs=[hbm, hbm] + [vmem] * 5,
-        out_specs=(vmem,) * 6,
-        scratch_shapes=scratch,
-        compiler_params=pltpu.CompilerParams(
-            collective_id=0, has_side_effects=True, vmem_limit_bytes=48 * 1024 * 1024
-        ),
-    )(
-        section_input.reshape(micros, height, width, channels),
-        adjoint_in.reshape(micros, height, width, channels),
-        kernel.reshape(TAPS, cpd).T,
-        conv_bias.reshape(1, cpd),
-        ln_gain.reshape(1, cpd),
-        ln_shift.reshape(1, cpd),
-        layer_scale.reshape(1, cpd),
-    )
-    adjoint, kgrad, bgrad, ggrad, sgrad, lgrad = found
+        in_specs=[hbm] + [vmem] * 4,
+        out_specs=(hbm,) + (vmem,) * 5,
+        scratch_shapes=[
+            pltpu.VMEM((micros, height, width, channels), BF16),
+            pltpu.VMEM((LANES, LANES), F32),
+            dma((2, micros)),
+        ],
+        compiler_params=pltpu.CompilerParams(vmem_limit_bytes=60 * 1024 * 1024),
+    )(whole, sums, *vectors[1:])
     return (
         adjoint.reshape(section_input.shape),
         kgrad.T.reshape(kernel.shape),

time: 89.6 us -> 82 us (0.915)
  the two profiles are of different devices: /device:TPU:8 before, /device:TPU:56 now
where the time goes in v3:
time: 82 us; the launch traced here: 81.7 us
  Pallas kernels  81.1 us (99%)
    pallas_call x1, Pallas kernels, local(): pl.pallas_call(functools.partial(body, (zs, xs_count, rows, cpd, chunks,...  78 us
    pallas_call x1, Pallas kernels, local(): pl.pallas_call(finish, out_shape=(jax.ShapeDtypeStruct((micros, height, w...  3.13 us

profile of v3, /device:TPU:56, one launch (start us, length us, event | category | flops | bytes accessed | tf_op | source)
XLA Modules:
  0.0 81.7 jit_solution(15528290989602464929)
XLA Ops:
  0.6 78.0 %shard_map.118 = (bf16[2,5,16,1536]{3,2,1,0:T(8,128)(2,1)}, f32[24,128]{1,0:T(8,128)}) custom-call(bf16[2,5,16,1536]{3,2,1,0:T(8,128)(2,1)} %bitcast.19, bf16[2,5,16,1536]{3,2,1,0:T(8,128)(2,1)} %bitcast.20, bf16[24,49]{1,0:T(8,128)(2,1)} %bitcast.21, bf16[1,24]{1,0:T(2,128)(2,1)} %bitcast.28, bf16[1,24]{1,0:T(2,128)(2,1)} %bitcast.22, ...), custom_call_target="tpu_custom_call" | custom-call | tf_op jit(solution)/shard_map/pallas_call | solution.py:698
  78.6 3.1 %shard_map.119 = (bf16[2,5,16,1536]{3,2,1,0:T(8,128)(2,1)}, f32[24,49]{1,0:T(8,128)}, f32[1,24]{1,0:T(1,128)}, f32[1,24]{1,0:T(1,128)}, f32[1,24]{1,0:T(1,128)}, /*index=5*/f32[1,24]{1,0:T(1,128)}) custom-call(bf16[2,5,16,1536]{3,2,1,0:T(8,128)(2,1)} %get-tuple-element.14.whole_ref, f32[24,128]{1,0:T(8,128)} %get-tuple-element.15.sums_ref, ...), custom_call_target="tpu_custom_call" | custom-call | tf_op jit(solution)/shard_map/pallas_call | solution.py:716

commit v4 on v3

--- a/solution.py
+++ b/solution.py
@@ -17,6 +17,7 @@
 XS = 4
 TAPS = 49
 BIAS, GAIN, SHIFT, SCALE = 49, 50, 51, 52
+BLOCKS = 3
 SUM_G, SUM_GN, SUM_MIX = 49, 50, 51
 
 
@@ -169,11 +170,29 @@
     def x_up(s):
         return remote(xbuf.at[s, 0:3], xhalo.at[s, 1], xh_send.at[s, 1], xh_recv.at[s, 1], rows=(row + rows - 1) % rows)
 
-    def g_down(s):
-        return remote(gmix.at[s, height - 3 : height], ghalo.at[s, 0], gh_send.at[s, 0], gh_recv.at[s, 0], rows=(row + 1) % rows)
-
-    def g_up(s):
-        return remote(gmix.at[s, 0:3], ghalo.at[s, 1], gh_send.at[s, 1], gh_recv.at[s, 1], rows=(row + rows - 1) % rows)
+    block_chunks = chunks // BLOCKS
+    block_lanes = block_chunks * LANES
+
+    def block_of(b):
+        return pl.ds(pl.multiple_of(b * block_lanes, LANES), block_lanes)
+
+    def g_down(s, b):
+        return remote(
+            gmix.at[s, height - 3 : height, :, block_of(b)],
+            ghalo.at[s, 0, :, :, block_of(b)],
+            gh_send.at[s, 0, b],
+            gh_recv.at[s, 0, b],
+            rows=(row + 1) % rows,
+        )
+
+    def g_up(s, b):
+        return remote(
+            gmix.at[s, 0:3, :, block_of(b)],
+            ghalo.at[s, 1, :, :, block_of(b)],
+            gh_send.at[s, 1, b],
+            gh_recv.at[s, 1, b],
+            rows=(row + rows - 1) % rows,
+        )
 
     @pl.when(row < rows - 1)
     def _():
@@ -272,19 +291,20 @@
     over_z(half)
     lax.fori_loop(0, chunks, clear, 0)
     over_x(half)
+    swapped.wait_recv()
+    over_z(other)
     own_x.wait()
     widen(half)
     over_core(half)
-    swapped.wait_recv()
-    over_z(other)
+    over_x(other)
     settle(half)
 
-    def put_halo(pad, halo, s, side, start):
+    def put_halo(pad, halo, s, side, start, first=0, count=chunks):
         def one(ch, carry):
             pad[s, ch, start : start + 3, OFF : OFF + width, :] = halo[s, side, :, :, lanes_of(ch)].astype(F32)
             return carry
 
-        lax.fori_loop(0, chunks, one, 0)
+        lax.fori_loop(first, first + count, one, 0)
 
     def par(s, ch, which):
         return weights[s, ch, which : which + 1, :][None]
@@ -337,10 +357,6 @@
         variance = jnp.sum(squares, axis=-1, keepdims=True) * inverse_count
         inverse = lax.rsqrt(variance + EPSILON)
         stats[s, 1] = jnp.broadcast_to(inverse, (height, width, LANES))
-
-        @pl.when(s == half)
-        def _():
-            over_x(other)
 
     def folded(value):
         flat_rows = jnp.sum(value, axis=0)
@@ -383,36 +399,43 @@
             kacc[ch, SUM_MIX] = folded(again)
             return carry
 
-        lax.fori_loop(0, chunks, second, 0)
-
-        @pl.when(row < rows - 1)
-        def _():
-            g_down(s).start()
-
-        @pl.when(row > 0)
-        def _():
-            g_up(s).start()
+        def part(b, carry):
+            lax.fori_loop(b * block_chunks, (b + 1) * block_chunks, second, 0)
+
+            @pl.when(row < rows - 1)
+            def _():
+                g_down(s, b).start()
+
+            @pl.when(row > 0)
+            def _():
+                g_up(s, b).start()
+
+            return carry
+
+        lax.fori_loop(0, BLOCKS, part, 0)
 
     def keep_out(s):
         return pltpu.make_async_copy(gbuf.at[1 - s], out_ref.at[half], local_sem.at[2])
 
-    def send_out(s):
-        return remote(gbuf.at[1 - s], out_ref.at[half], back_send.at[0], back_recv.at[0], segment=other)
-
-    def out_arrival():
-        return remote(gbuf.at[0], out_ref.at[other], back_send.at[0], back_recv.at[0], segment=other)
+    def send_out(s, b):
+        return remote(
+            gbuf.at[1 - s, :, :, block_of(b)],
+            out_ref.at[half, :, :, block_of(b)],
+            back_send.at[b],
+            back_recv.at[b],
+            segment=other,
+        )
+
+    def out_arrival(b):
+        return remote(
+            gbuf.at[0, :, :, block_of(b)],
+            out_ref.at[other, :, :, block_of(b)],
+            back_send.at[b],
+            back_recv.at[b],
+            segment=other,
+        )
 
     def adjoint(s):
-        @pl.when(row > 0)
-        def _():
-            g_down(s).wait_recv()
-            put_halo(gpad, ghalo, s, 0, 0)
-
-        @pl.when(row < rows - 1)
-        def _():
-            g_up(s).wait_recv()
-            put_halo(gpad, ghalo, s, 1, 3 + height)
-
         def conv(ch, carry):
             acc = gbuf[s, :, :, lanes_of(ch)].astype(F32)
             for c in range(7):
@@ -422,15 +445,32 @@
             gbuf[1 - s, :, :, lanes_of(ch)] = acc.astype(BF16)
             return carry
 
-        lax.fori_loop(0, chunks, conv, 0)
+        def part(b, carry):
+            first = b * block_chunks
+
+            @pl.when(row > 0)
+            def _():
+                g_down(s, b).wait_recv()
+                put_halo(gpad, ghalo, s, 0, 0, first, block_chunks)
+
+            @pl.when(row < rows - 1)
+            def _():
+                g_up(s, b).wait_recv()
+                put_halo(gpad, ghalo, s, 1, 3 + height, first, block_chunks)
+
+            lax.fori_loop(first, first + block_chunks, conv, 0)
+
+            @pl.when(s != half)
+            def _():
+                send_out(s, b).start()
+
+            return carry
+
+        lax.fori_loop(0, BLOCKS, part, 0)
 
         @pl.when(s == half)
         def _():
             keep_out(s).start()
-
-        @pl.when(s != half)
-        def _():
-            send_out(s).start()
 
     def r1_copy(s, k):
         to = (xc + k) % xcs
@@ -469,7 +509,7 @@
             r1_copy(s, k).start()
 
     ARRIVE, FORWARD, NORM, TAPS_OF, ADJOINT, OVER_CORE, SETTLE = range(7)
-    lower = ((FORWARD, 0), (ARRIVE, 1), (OVER_CORE, 1), (SETTLE, 1), (FORWARD, 1), (NORM, 1), (TAPS_OF, 1))
+    lower = ((ARRIVE, 1), (FORWARD, 0), (OVER_CORE, 1), (SETTLE, 1), (FORWARD, 1), (NORM, 1), (TAPS_OF, 1))
     upper = ((FORWARD, 1), (NORM, 1), (OVER_CORE, 0), (ARRIVE, 0), (TAPS_OF, 1), (SETTLE, 0), (FORWARD, 0))
     common = ((ADJOINT, 1), (NORM, 0), (TAPS_OF, 0), (ADJOINT, 0))
     acts = (arrive, forward, norm_back, taps, adjoint, over_core, settle)
@@ -580,12 +620,14 @@
         @pl.when(row < rows - 1)
         def _():
             x_down(s).wait_send()
-            g_down(s).wait_send()
+            for b in range(BLOCKS):
+                g_down(s, b).wait_send()
 
         @pl.when(row > 0)
         def _():
             x_up(s).wait_send()
-            g_up(s).wait_send()
+            for b in range(BLOCKS):
+                g_up(s, b).wait_send()
 
         for k in range(1, xcs):
             r1_copy(s, k).wait_send()
@@ -606,8 +648,9 @@
             else:
                 r3_copy(part, k).wait_send()
     keep_out(0).wait()
-    send_out(0).wait_send()
-    out_arrival().wait_recv()
+    for b in range(BLOCKS):
+        send_out(0, b).wait_send()
+        out_arrival(b).wait_recv()
 
 
 def finish(whole_ref, sums_ref, gain_ref, shift_ref, scale_ref, out_ref, kgrad_ref, bgrad_ref, ggrad_ref, sgrad_ref, lgrad_ref, held, stage, sem):
@@ -683,10 +726,10 @@
         dma((1,)),
         dma((2, 2)),
         dma((2, 2)),
-        dma((2, 2)),
-        dma((2, 2)),
-        dma((1,)),
-        dma((1,)),
+        dma((2, 2, BLOCKS)),
+        dma((2, 2, BLOCKS)),
+        dma((BLOCKS,)),
+        dma((BLOCKS,)),
         dma((2, xcs)),
         dma((2, xcs)),
         dma((2, rows)),

time: 82 us -> 76.4 us (0.932)
  the two profiles are of different devices: /device:TPU:56 before, /device:TPU:16 now
where the time goes in v4:
time: 76.4 us; the launch traced here: 76.2 us
  Pallas kernels  75.6 us (99%)
    pallas_call x1, Pallas kernels, local(): pl.pallas_call(functools.partial(body, (zs, xs_count, rows, cpd, chunks,...  72.4 us
    pallas_call x1, Pallas kernels, local(): pl.pallas_call(finish, out_shape=(jax.ShapeDtypeStruct((micros, height, w...  3.13 us

profile of v4, /device:TPU:16, one launch (start us, length us, event | category | flops | bytes accessed | tf_op | source)
XLA Modules:
  0.0 76.2 jit_solution(5819790746817153098)
XLA Ops:
  0.6 72.4 %shard_map.118 = (bf16[2,5,16,1536]{3,2,1,0:T(8,128)(2,1)}, f32[24,128]{1,0:T(8,128)}) custom-call(bf16[2,5,16,1536]{3,2,1,0:T(8,128)(2,1)} %bitcast.19, bf16[2,5,16,1536]{3,2,1,0:T(8,128)(2,1)} %bitcast.20, bf16[24,49]{1,0:T(8,128)(2,1)} %bitcast.21, bf16[1,24]{1,0:T(2,128)(2,1)} %bitcast.28, bf16[1,24]{1,0:T(2,128)(2,1)} %bitcast.22, ...), custom_call_target="tpu_custom_call" | custom-call | tf_op jit(solution)/shard_map/pallas_call | solution.py:741
  73.1 3.1 %shard_map.119 = (bf16[2,5,16,1536]{3,2,1,0:T(8,128)(2,1)}, f32[24,49]{1,0:T(8,128)}, f32[1,24]{1,0:T(1,128)}, f32[1,24]{1,0:T(1,128)}, f32[1,24]{1,0:T(1,128)}, /*index=5*/f32[1,24]{1,0:T(1,128)}) custom-call(bf16[2,5,16,1536]{3,2,1,0:T(8,128)(2,1)} %get-tuple-element.14.whole_ref, f32[24,128]{1,0:T(8,128)} %get-tuple-element.15.sums_ref, ...), custom_call_target="tpu_custom_call" | custom-call | tf_op jit(solution)/shard_map/pallas_call | solution.py:759

commit v5 on v4

--- a/solution.py
+++ b/solution.py
@@ -503,8 +503,11 @@
         for ch in range(middle):
             joined = jnp.concatenate([terms[ch], terms[middle + ch]], axis=0)
             flat[ch * LANES : (ch + 1) * LANES, :] = jnp.transpose(joined)
-        for d in range(rows * xcs):
-            pieces[s, d // xcs, d % xcs] = flat[d * cpd : (d + 1) * cpd, :]
+        for pair in range(rows // 2):
+            for to in range(xcs):
+                owners = [(2 * pair + at) * xcs + to for at in range(2)]
+                joined = jnp.concatenate([flat[d * cpd : (d + 1) * cpd, :] for d in owners], axis=0)
+                pieces[s, pair, to] = joined.astype(BF16)
         for k in range(1, xcs):
             r1_copy(s, k).start()
 
@@ -548,10 +551,11 @@
         for k in range(1, xcs):
             r1_arrival(s, k).wait_recv()
         got1[s, xc] = pieces[s, :, xc]
-        acc = got1[s, 0]
+        acc = got1[s, 0].astype(F32)
         for k in range(1, xcs):
-            acc = acc + got1[s, k]
-        sum1[s] = acc
+            acc = acc + got1[s, k].astype(F32)
+        for at in range(rows):
+            sum1[s, at] = acc[at // 2, at % 2 * cpd : (at % 2 + 1) * cpd]
 
         @pl.when(half == s)
         def _():
@@ -707,8 +711,8 @@
         pltpu.VMEM((chunks, TAPS + 3, 8, LANES), F32),
         pltpu.VMEM((chunks, 64, LANES), F32),
         pltpu.VMEM((channels // 2, LANES), F32),
-        pltpu.VMEM((2, rows, xcs, cpd, LANES), F32),
-        pltpu.VMEM((2, xcs, rows, cpd, LANES), F32),
+        pltpu.VMEM((2, rows // 2, xcs, 2 * cpd, LANES), BF16),
+        pltpu.VMEM((2, xcs, rows // 2, 2 * cpd, LANES), BF16),
         pltpu.VMEM((2, rows, cpd, LANES), F32),
         pltpu.VMEM((2, rows, cpd, LANES), F32),
         pltpu.VMEM((cpd, LANES), F32),

time: 76.4 us -> 76.1 us (level)
  the two profiles are of different devices: /device:TPU:16 before, /device:TPU:8 now
where the time goes in v5:
time: 76.1 us; the launch traced here: 75.8 us
  Pallas kernels  75.2 us (99%)
    pallas_call x1, Pallas kernels, local(): pl.pallas_call(functools.partial(body, (zs, xs_count, rows, cpd, chunks,...  72.1 us
    pallas_call x1, Pallas kernels, local(): pl.pallas_call(finish, out_shape=(jax.ShapeDtypeStruct((micros, height, w...  3.13 us

profile of v5, /device:TPU:8, one launch (start us, length us, event | category | flops | bytes accessed | tf_op | source)
XLA Modules:
  0.0 75.8 jit_solution(225916064239392828)
XLA Ops:
  0.6 72.1 %shard_map.118 = (bf16[2,5,16,1536]{3,2,1,0:T(8,128)(2,1)}, f32[24,128]{1,0:T(8,128)}) custom-call(bf16[2,5,16,1536]{3,2,1,0:T(8,128)(2,1)} %bitcast.19, bf16[2,5,16,1536]{3,2,1,0:T(8,128)(2,1)} %bitcast.20, bf16[24,49]{1,0:T(8,128)(2,1)} %bitcast.21, bf16[1,24]{1,0:T(2,128)(2,1)} %bitcast.28, bf16[1,24]{1,0:T(2,128)(2,1)} %bitcast.22, ...), custom_call_target="tpu_custom_call" | custom-call | tf_op jit(solution)/shard_map/pallas_call | solution.py:745
  72.7 3.1 %shard_map.119 = (bf16[2,5,16,1536]{3,2,1,0:T(8,128)(2,1)}, f32[24,49]{1,0:T(8,128)}, f32[1,24]{1,0:T(1,128)}, f32[1,24]{1,0:T(1,128)}, f32[1,24]{1,0:T(1,128)}, /*index=5*/f32[1,24]{1,0:T(1,128)}) custom-call(bf16[2,5,16,1536]{3,2,1,0:T(8,128)(2,1)} %get-tuple-element.14.whole_ref, f32[24,128]{1,0:T(8,128)} %get-tuple-element.15.sums_ref, ...), custom_call_target="tpu_custom_call" | custom-call | tf_op jit(solution)/shard_map/pallas_call | solution.py:763
